TPU v7x, 32 devices: a whole 2x2x4 slice. The times are simulated.
32 devices in a mesh: pipe: 4 (over y, x), dp: 8 (over z, core).
Axes of the slice: x: 2, y: 2, z: 4, core: 2. Of those that a mesh axis runs over, the one named last changes fastest.
Arguments:
- new_input: bfloat16 [4, 1024, 8192], P('pipe', 'dp'), may hold values from -400 to 400
- new_gain: bfloat16 [4, 8192], P('pipe'), may hold values from 0.5 to 1.5
- queries: bfloat16 [4, 1024, 4096], P('pipe', 'dp'), may hold values from -5 to 5
- new_keys: bfloat16 [4, 1024, 512], P('pipe', 'dp'), may hold values from -5 to 5
- context_grad: bfloat16 [4, 1024, 4096], P('pipe', 'dp'), may hold values from -0.08984375 to 0.08984375
- segment_ids: int32 [4, 1024], P('pipe', 'dp'), may hold values from 0 to 15, never falling along the last dimension, each value on 1 to 128 neighbouring positions
- frozen_input: bfloat16 [4, 1024, 8192], P('pipe', 'dp'), may hold values from -400 to 400
- frozen_gain: bfloat16 [4, 8192], P('pipe'), may hold values from 0.5 to 1.5
- output_grad: bfloat16 [4, 1024, 8192], P('pipe', 'dp'), may hold values from -6 to 6
- kv_grad: bfloat16 [4, 1024, 1024], P('pipe', 'dp'), may hold values from -18 to 18
- kv_weight: bfloat16 [4, 8192, 1024], P('pipe', 'dp'), may hold values from -0.0625 to 0.0625
Outputs:
- cot_below: bfloat16 [4, 1024, 8192], P('pipe', 'dp')
- value_grad: float32 [4, 8192, 512], P('pipe', 'dp')
Inputs may be any that keep to these rules, and one draw needn't show every extreme that they name: `segment_ids`: within a section the numbers never fall; every number of 0 to 15 appears, on 1 to 128 positions in a row, one on exactly 128.
All inputs are finite; a program needn't handle non-finite values.
Results may differ from a plain program's by a relative error of at most 0.0056.
Values may be sent and summed in bfloat16 or wider, within the bound.
No kernel may reach another device: no remote copies, remote signals or barrier semaphores. Data moves between devices by JAX's collectives and lax.ppermute only.
A program may use at most 128 MiB of HBM per device.

v0:
```python
import functools
import math

import jax
import jax.numpy as jnp
from jax import lax
from jax.experimental import pallas as pl
from jax.experimental.pallas import tpu as pltpu
from jax.sharding import PartitionSpec as P

HEAD = 128
CORES = 2
MIB = 1 << 20

norm_eps = 1e-05
masked_value = -1e30

whole = pl.BlockSpec(memory_space=pl.ANY)
scalars = pl.BlockSpec(memory_space=pltpu.SMEM)


def from_behind(array, axis, by):
    length = lax.axis_size(axis)
    pairs = [(i, i + by) for i in range(length) if 0 <= i + by < length]
    return lax.ppermute(array, axis, pairs)


def along_chips(array, by, first=0):
    length = lax.axis_size("dp")
    pairs = [
        (line * length + i, line * length + (i + by * CORES) % length)
        for line in range(first, lax.axis_size("pipe")) for i in range(length)
    ]
    return lax.ppermute(array, ("pipe", "dp"), pairs)


def between_lines(array, source, target):
    length = lax.axis_size("dp")
    pairs = [(source * length + i, target * length + i) for i in range(length)]
    return lax.ppermute(array, ("pipe", "dp"), pairs)


def on_line(array, by, line):
    length = lax.axis_size("dp")
    pairs = [(line * length + i, line * length + (i + by * CORES) % length) for i in range(length)]
    return lax.ppermute(array, ("pipe", "dp"), pairs)


def swap_cores(array):
    length = lax.axis_size("dp")
    return lax.ppermute(array, "dp", [(i, i ^ 1) for i in range(length)])


def call(body, name, flops, nbytes, vmem=24, **kwargs):
    return pl.pallas_call(
        body,
        name=name,
        compiler_params=pltpu.CompilerParams(vmem_limit_bytes=vmem * MIB),
        cost_estimate=pl.CostEstimate(flops=flops, bytes_accessed=nbytes, transcendentals=0),
        **kwargs,
    )


def part_columns(chip, half, core, width):
    owner = chip * CORES + (core if half == 0 else CORES - 1 - core)
    return pl.ds(pl.multiple_of(owner * width, width), width)


def norm_kernel(chips, ahead, place_ref, x_ref, gain_ref, cot_ref, *rest):
    out_refs = rest[-len(ahead):]
    chip, core = place_ref[0], place_ref[1]
    values = x_ref[...].astype(jnp.float32)
    inverse = lax.rsqrt(jnp.mean(values * values, axis=-1, keepdims=True) + norm_eps)
    front = cot_ref.shape[1]
    width = (out_refs[0].shape[1] - front) // CORES
    for by, out_ref in zip(ahead, out_refs):
        to = lax.rem(chip + by, chips)
        out_ref[:, :front] = cot_ref[...]
        for half in range(CORES):
            cols = part_columns(to, half, core, width)
            out_ref[:, front + half * width:front + (half + 1) * width] = (
                x_ref[:, cols].astype(jnp.float32) * inverse * gain_ref[:, cols].astype(jnp.float32)
            ).astype(out_ref.dtype)


def normalize(place, rows, gain, cot, chips, ahead, start, count, after):
    width = rows.shape[1]
    front = cot.shape[1]
    block = math.gcd(math.gcd(start, count), 32)
    first = start // block
    out_width = front + width // chips
    return list(call(
        functools.partial(norm_kernel, chips, ahead), "norm_forward",
        4 * count * width, 2 * count * width + 2 * count * out_width * len(ahead),
        grid=(count // block,),
        in_specs=[
            scalars,
            pl.BlockSpec((block, width), lambda i: (first + i, 0)),
            pl.BlockSpec((1, width), lambda i: (0, 0)),
            pl.BlockSpec((block, front), lambda i: (first + i, 0)),
        ] + [whole] * len(after),
        out_specs=[pl.BlockSpec((block, out_width), lambda i: (i, 0))] * len(ahead),
        out_shape=[jax.ShapeDtypeStruct((count, out_width), jnp.bfloat16)] * len(ahead),
    )(place, rows, gain, cot, *after))


def stack_kernel(count, *refs):
    at = 0
    for ref in refs[:count]:
        refs[-1][at:at + ref.shape[0]] = ref[...]
        at += ref.shape[0]


def stack_rows(arrays, after):
    width = arrays[0].shape[1]
    tall = sum(array.shape[0] for array in arrays)
    return call(
        functools.partial(stack_kernel, len(arrays)), "stack_rows", 0, 4 * tall * width,
        grid=(1,),
        in_specs=[pl.BlockSpec(array.shape, lambda i: (0, 0)) for array in arrays] + [whole] * len(after),
        out_specs=pl.BlockSpec((tall, width), lambda i: (0, 0)),
        out_shape=jax.ShapeDtypeStruct((tall, width), arrays[0].dtype),
    )(*arrays, *after)


def attend_kernel(query_ref, key_ref, grad_ref, row_seg_ref, col_seg_ref, out_ref):
    tokens = key_ref.shape[0]
    group = query_ref.shape[1] // HEAD
    at_query = lax.broadcasted_iota(jnp.int32, (tokens, tokens), 0)
    at_key = lax.broadcasted_iota(jnp.int32, (tokens, tokens), 1)
    visible = (col_seg_ref[...] == row_seg_ref[...]) & (at_key <= at_query)
    keys = key_ref[...]
    total = jnp.zeros((tokens, HEAD), jnp.float32)
    for head in range(group):
        cols = slice(head * HEAD, (head + 1) * HEAD)
        scores = lax.dot_general(
            query_ref[:, cols], keys, (((1,), (1,)), ((), ())),
            preferred_element_type=jnp.float32,
        ) / math.sqrt(HEAD)
        masked = jnp.where(visible, scores, masked_value)
        highest = jnp.max(masked, axis=-1, keepdims=True)
        weights = jnp.where(visible, jnp.exp(masked - highest), 0.0)
        attention = (weights / jnp.sum(weights, axis=-1, keepdims=True)).astype(jnp.bfloat16)
        total += lax.dot_general(
            attention, grad_ref[:, cols], (((0,), (0,)), ((), ())),
            preferred_element_type=jnp.float32,
        )
    out_ref[...] = total.astype(out_ref.dtype)


def attend(queries, keys, grads, segments):
    tokens, kv_width = keys.shape
    heads = kv_width // HEAD
    wide = queries.shape[1] // heads
    return call(
        attend_kernel, "attend",
        4 * tokens * tokens * queries.shape[1], 4 * tokens * queries.shape[1],
        grid=(heads,),
        in_specs=[
            pl.BlockSpec((tokens, wide), lambda i: (0, i)),
            pl.BlockSpec((tokens, HEAD), lambda i: (0, i)),
            pl.BlockSpec((tokens, wide), lambda i: (0, i)),
            pl.BlockSpec((1, tokens), lambda i: (0, 0)),
            pl.BlockSpec((tokens, 1), lambda i: (0, 0)),
        ],
        out_specs=pl.BlockSpec((tokens, HEAD), lambda i: (0, i)),
        out_shape=jax.ShapeDtypeStruct((tokens, kv_width), jnp.bfloat16),
    )(queries, keys, grads, segments, segments.reshape(tokens, 1))


def project_kernel(chips, steps, own_ref, other_ref, *rest):
    row_refs, out_refs, gathered = rest[:chips], rest[-chips - 1:-1], rest[-1]
    taken, depth = row_refs[0].shape
    step = pl.program_id(0)

    @pl.when(step == 0)
    def _():
        for by in range(chips):
            gathered[by] = row_refs[by][...]

    def multiply(weight_ref):
        product = lax.dot_general(
            gathered[...].reshape(chips * taken, depth), weight_ref[...], (((1,), (1,)), ((), ())),
            preferred_element_type=jnp.float32,
        ).astype(jnp.bfloat16)
        for by in range(chips):
            out_refs[by][...] = product[by * taken:(by + 1) * taken]

    @pl.when(step < steps)
    def _():
        multiply(own_ref)

    @pl.when(step >= steps)
    def _():
        multiply(other_ref)


def project(rows, own, other, after):
    chips = len(rows)
    taken, depth = rows[0].shape
    width = own.shape[0]
    block = min(width, 256)
    steps = width // block
    return call(
        functools.partial(project_kernel, chips, steps), "project",
        4 * chips * taken * depth * width, 2 * (chips * taken * (depth + 2 * width) + 2 * width * depth),
        grid=(CORES * steps,),
        in_specs=[
            pl.BlockSpec((block, depth), lambda i: (jnp.minimum(i, steps - 1), 0)),
            pl.BlockSpec((block, depth), lambda i: (jnp.maximum(i - steps, 0), 0)),
        ] + [pl.BlockSpec((taken, depth), lambda i: (0, 0))] * chips + [whole] * len(after),
        out_specs=[pl.BlockSpec((taken, block), lambda i: (0, i))] * chips,
        out_shape=[jax.ShapeDtypeStruct((taken, CORES * width), jnp.bfloat16)] * chips,
        scratch_shapes=[pltpu.VMEM((chips, taken, depth), jnp.bfloat16)],
    )(own, other, *rows, *after)


def backward_kernel(chips, place_ref, x_ref, gain_ref, grad_ref, *rest):
    cot_refs, out_ref = rest[:chips], rest[-1]
    chip, core = place_ref[0], place_ref[1]
    values = x_ref[...].astype(jnp.float32)
    width = cot_refs[0].shape[1] // CORES
    inverse = lax.rsqrt(jnp.mean(values * values, axis=-1, keepdims=True) + norm_eps)
    inner = jnp.zeros_like(inverse)

    def parts():
        for by, cot_ref in enumerate(cot_refs):
            source = lax.rem(chip + chips - by, chips)
            for half in range(CORES):
                cols = part_columns(source, half, core, width)
                cot = cot_ref[:, half * width:(half + 1) * width].astype(jnp.float32)
                yield cols, gain_ref[:, cols].astype(jnp.float32) * cot

    for cols, scaled in parts():
        inner += jnp.sum(x_ref[:, cols].astype(jnp.float32) * scaled, axis=-1, keepdims=True)
    factor = inverse * inverse * inverse * (inner / x_ref.shape[1])
    for cols, scaled in parts():
        out_ref[:, cols] = (
            grad_ref[:, cols].astype(jnp.float32)
            + inverse * scaled
            - x_ref[:, cols].astype(jnp.float32) * factor
        ).astype(out_ref.dtype)


def norm_backward(place, cots, rows, gain, grads, after):
    tokens, width = rows.shape
    taken, part_width = cots[0].shape
    block = min(taken, 32)
    return call(
        functools.partial(backward_kernel, len(cots)), "norm_backward",
        10 * taken * width, 8 * taken * width,
        grid=(taken // block,),
        in_specs=[
            scalars,
            pl.BlockSpec((block, width), lambda i: (i, 0)),
            pl.BlockSpec((1, width), lambda i: (0, 0)),
            pl.BlockSpec((block, width), lambda i: (i, 0)),
        ] + [pl.BlockSpec((block, part_width), lambda i: (i, 0))] * len(cots) + [whole] * len(after),
        out_specs=pl.BlockSpec((block, width), lambda i: (i, 0)),
        out_shape=jax.ShapeDtypeStruct((taken, width), jnp.bfloat16),
    )(place, rows, gain, grads, *cots, *after)


def outer_kernel(groups, sums, *refs):
    arrays = sum(groups)
    cots, columns, terms = refs[:arrays], refs[arrays:2 * arrays], refs[2 * arrays:2 * arrays + sums]
    total, at = None, 0
    for size in groups:
        column, cot = columns[at][...], cots[at][...]
        for more in range(at + 1, at + size):
            column, cot = column + columns[more][...], cot + cots[more][...]
        at += size
        product = lax.dot_general(
            column, cot, (((0,), (0,)), ((), ())), preferred_element_type=jnp.float32
        )
        total = product if total is None else total + product
    for term in terms:
        total += term[...].astype(jnp.float32)
    refs[-1][...] = total.astype(refs[-1].dtype)


def outer(groups, cot_width, half, before, dtype):
    payloads = [payload for group in groups for payload in group]
    wide = payloads[0].shape[1]
    width = (wide - cot_width) // CORES
    block = math.gcd(math.gcd(width, 256), cot_width)
    first = (cot_width + half * width) // block
    out_spec = pl.BlockSpec((block, cot_width), lambda i: (i, 0))
    tokens = sum(payload.shape[0] for payload in payloads)
    return call(
        functools.partial(outer_kernel, [len(group) for group in groups], len(before)), "outer",
        2 * tokens * width * cot_width, 2 * tokens * width + 4 * width * cot_width,
        grid=(width // block,),
        in_specs=[pl.BlockSpec((payload.shape[0], cot_width), lambda i: (0, 0)) for payload in payloads]
        + [pl.BlockSpec((payload.shape[0], block), lambda i: (0, first + i)) for payload in payloads]
        + [out_spec] * len(before),
        out_specs=out_spec,
        out_shape=jax.ShapeDtypeStruct((width, cot_width), dtype),
    )(*payloads, *payloads, *before)


def shards(
    new_input,
    new_gain,
    queries,
    new_keys,
    context_grad,
    segment_ids,
    frozen_input,
    frozen_gain,
    output_grad,
    kv_grad,
    kv_weight,
):
    chips = lax.axis_size("dp") // CORES
    sections = lax.axis_size("pipe")
    tokens, kv_width = new_keys.shape[1:]
    at = lax.axis_index("dp")
    place = jnp.stack([at // CORES, at % CORES]).astype(jnp.int32)
    middle = chips // 2
    near = [by for by in range(1, chips) if by != middle]
    spread = tokens // 4

    rows = [kv_grad[0]] + [along_chips(kv_grad[0], chips - by, 1) for by in range(1, chips)]
    other_weight = swap_cores(kv_weight[0])
    value_cot = attend(queries[0], new_keys[0], context_grad[0], segment_ids)

    apply = functools.partial(normalize, place, new_input[0], new_gain, value_cot, chips)
    shared = apply([middle], 0, spread, [other_weight])[0]
    brought = [between_lines(shared, section, 0) for section in range(1, sections)]
    early = apply([0] + near[:1], 0, tokens, rows[1:])
    columns = [early[0]] + [along_chips(block, by) for block, by in zip(early[1:], near)]
    joint = stack_rows([shared] + brought, early[:1])
    moved = on_line(joint, middle, 0)
    returned = [moved[:spread]] + [
        between_lines(moved[section * spread:(section + 1) * spread], 0, section) for section in range(1, sections)
    ]

    parts = project(rows, kv_weight[0], other_weight, [joint])
    arrived = [parts[0]] + [along_chips(parts[by], by, 1) for by in range(1, chips)]
    kept = apply([middle], spread, tokens - spread, [parts[0]])
    late = apply(near[1:], 0, tokens, kept)

    input_cot = norm_backward(
        place, arrived, frozen_input[0], frozen_gain, output_grad[0], late[:1] + returned[1:] + columns[1:]
    )
    cot_below = from_behind(input_cot, "pipe", -1)

    columns += [along_chips(block, by) for block, by in zip(late, near[1:])]
    last = along_chips(kept[0], middle)

    groups = [[column] for column in columns] + [returned]
    sums = [outer(groups, kv_width, half, [], jnp.float32) for half in range(CORES)]
    given = outer([[last]], kv_width, 1, [sums[1]], jnp.bfloat16)
    taken = swap_cores(given)
    grad = outer([[last]], kv_width, 0, [sums[0], taken], jnp.float32)
    return (cot_below[None], grad[None])


def solution(mesh):
    placed = (
        P("pipe", "dp", None),
        P("pipe", None),
        P("pipe", "dp", None),
        P("pipe", "dp", None),
        P("pipe", "dp", None),
        P("pipe", "dp"),
        P("pipe", "dp", None),
        P("pipe", None),
        P("pipe", "dp", None),
        P("pipe", "dp", None),
        P("pipe", "dp", None),
    )
    return jax.shard_map(
        shards,
        mesh=mesh,
        in_specs=placed,
        out_specs=(P("pipe", "dp", None), P("pipe", "dp", None)),
        check_vma=False,
    )
```

profile of v0, /device:TPU:10, one launch (start us, length us, event | category | flops | bytes accessed | tf_op | source)
XLA Modules:
  0.0 148.1 jit_solution(8189342227903744675)
XLA Ops:
  0.6 0.1 collective-permute-start
  0.7 3.6 %collective-permute-start.3 = (bf16[128,1024]{1,0:T(8,128)(2,1)}, bf16[128,1024]{1,0:T(8,128)(2,1)S(1)}, u32[]{:S(2)}, u32[]{:S(2)}) collective-permute-start(bf16[128,1024]{1,0:T(8,128)(2,1)} %bitcast.25), channel_id=1, source_target_pairs={{8,10},{9,11},{10,12},{11,13},{12,14},{13,15},{14,8},{15,9},{16,18... | collective-permute-start | bytes 786440 | tf_op jit(solution)/shard_map/ppermute | solution.py:34
  4.3 3.1 %collective-permute-start.2 = (bf16[128,1024]{1,0:T(8,128)(2,1)}, bf16[128,1024]{1,0:T(8,128)(2,1)S(1)}, u32[]{:S(2)}, u32[]{:S(2)}) collective-permute-start(bf16[128,1024]{1,0:T(8,128)(2,1)} %bitcast.26), channel_id=1, source_target_pairs={{8,12},{9,13},{10,14},{11,15},{12,8},{13,9},{14,10},{15,11},{16,20... | collective-permute-start | bytes 786440 | tf_op jit(solution)/shard_map/ppermute | solution.py:34
  7.5 3.7 %collective-permute-start.1 = (bf16[128,1024]{1,0:T(8,128)(2,1)}, bf16[128,1024]{1,0:T(8,128)(2,1)S(1)}, u32[]{:S(2)}, u32[]{:S(2)}) collective-permute-start(bf16[128,1024]{1,0:T(8,128)(2,1)} %bitcast.27), channel_id=1, source_target_pairs={{8,14},{9,15},{10,8},{11,9},{12,10},{13,11},{14,12},{15,13},{16,22... | collective-permute-start | bytes 786440 | tf_op jit(solution)/shard_map/ppermute | solution.py:34
  11.2 0.8 copy.13.col_seg_ref
  12.0 1.2 copy-done.3
  13.2 1.2 copy-done.4
  14.5 0.9 copy-done.6
  15.4 0.7 copy-done.8
  16.0 4.5 %attend.1.cot_ref = bf16[128,512]{1,0:T(8,128)(2,1)S(1)} custom-call(bf16[128,4096]{1,0:T(8,128)(2,1)S(1)} %bitcast.19, bf16[128,512]{1,0:T(8,128)(2,1)S(1)} %bitcast.21, bf16[128,4096]{1,0:T(8,128)(2,1)S(1)} %bitcast.20, s32[1,128]{1,0:T(1,128)S(1)} %copy-done.8, s32[128,1]{1,0:T(8,128)S(1)} %copy.13.col_seg_ref), custom_call_target="tpu_custom_call" | custom-call | flops 268435456 | bytes 2097152 | tf_op jit(solution)/shard_map/attend/pallas_call | solution.py:155
  20.5 0.1 pad_add_fusion.place_ref
  20.6 0.8 norm_forward.4.refs_0_
  21.4 0.0 copy-start.9
  21.4 0.8 collective-permute-start.6
  22.2 0.7 collective-permute-start.5
  22.9 1.3 collective-permute-start.4
  24.2 3.4 %collective-permute-done.2.rest_1_.rest_2_ = bf16[128,1024]{1,0:T(8,128)(2,1)S(1)} collective-permute-done((bf16[128,1024]{1,0:T(8,128)(2,1)}, bf16[128,1024]{1,0:T(8,128)(2,1)S(1)}, u32[]{:S(2)}, u32[]{:S(2)}) %collective-permute-start.2) | collective-permute-done | bytes 262176 | tf_op jit(solution)/shard_map/ppermute | solution.py:34
  27.6 1.7 %collective-permute-done.1.rest_0_.rest_1_ = bf16[128,1024]{1,0:T(8,128)(2,1)S(1)} collective-permute-done((bf16[128,1024]{1,0:T(8,128)(2,1)}, bf16[128,1024]{1,0:T(8,128)(2,1)S(1)}, u32[]{:S(2)}, u32[]{:S(2)}) %collective-permute-start.1) | collective-permute-done | bytes 262176 | tf_op jit(solution)/shard_map/ppermute | solution.py:34
  29.3 1.5 %norm_forward.5 = (bf16[128,2560]{1,0:T(8,128)(2,1)S(1)}, bf16[128,2560]{1,0:T(8,128)(2,1)S(1)}) custom-call(s32[2]{0:T(128)S(1)} %pad_add_fusion.place_ref, bf16[128,8192]{1,0:T(8,128)(2,1)S(1)} %bitcast.14, bf16[1,8192]{1,0:T(2,128)(2,1)S(1)} %copy-done.5, bf16[128,512]{1,0:T(8,128)(2,1)S(1)} %attend.1.cot_ref, ...), custom_call_target="tpu_custom_call" | custom-call | flops 4194304 | bytes 3407872 | tf_op jit(solution)/shard_map/norm_forward/pallas_call | solution.py:92
  30.9 0.7 collective-permute-start.10
  31.6 0.1 collective-permute-start.14
  31.7 6.4 %project.1 = (bf16[128,2048]{1,0:T(8,128)(2,1)S(1)}, bf16[128,2048]{1,0:T(8,128)(2,1)S(1)}, bf16[128,2048]{1,0:T(8,128)(2,1)S(1)}, bf16[128,2048]{1,0:T(8,128)(2,1)S(1)}) custom-call(bf16[1024,1024]{1,0:T(8,128)(2,1)S(1)} %bitcast.24, bf16[1024,1024]{1,0:T(8,128)(2,1)} %collective-permute-done.rest_0_.other_ref, bf16[128,1024]{1,0:T(8,128)(2,1)S(1)} %bitcast.28, ...), custom_call_target="tpu_custom_call" | custom-call | flops 2147483648 | bytes 7340032 | tf_op jit(solution)/shard_map/project/pallas_call | solution.py:204
  38.1 4.0 %collective-permute-start.7 = (bf16[128,2048]{1,0:T(8,128)(2,1)S(1)}, bf16[128,2048]{1,0:T(8,128)(2,1)S(1)}, u32[]{:S(2)}, u32[]{:S(2)}) collective-permute-start(bf16[128,2048]{1,0:T(8,128)(2,1)S(1)} %get-tuple-element.10), channel_id=1, source_target_pairs={{8,10},{9,11},{10,12},{11,13},{12,14},{13,15},{14,8},{15,9},{16,18... | collective-permute-start | bytes 1572872 | tf_op jit(solution)/shard_map/ppermute | solution.py:34
  42.1 4.2 %collective-permute-start.8 = (bf16[128,2048]{1,0:T(8,128)(2,1)S(1)}, bf16[128,2048]{1,0:T(8,128)(2,1)S(1)}, u32[]{:S(2)}, u32[]{:S(2)}) collective-permute-start(bf16[128,2048]{1,0:T(8,128)(2,1)S(1)} %get-tuple-element.11), channel_id=1, source_target_pairs={{8,12},{9,13},{10,14},{11,15},{12,8},{13,9},{14,10},{15,11},{16,20... | collective-permute-start | bytes 1572872 | tf_op jit(solution)/shard_map/ppermute | solution.py:34
  46.3 1.9 %collective-permute-start.9 = (bf16[128,2048]{1,0:T(8,128)(2,1)S(1)}, bf16[128,2048]{1,0:T(8,128)(2,1)S(1)}, u32[]{:S(2)}, u32[]{:S(2)}) collective-permute-start(bf16[128,2048]{1,0:T(8,128)(2,1)S(1)} %get-tuple-element.12), channel_id=1, source_target_pairs={{8,14},{9,15},{10,8},{11,9},{12,10},{13,11},{14,12},{15,13},{16,22... | collective-permute-start | bytes 1572872 | tf_op jit(solution)/shard_map/ppermute | solution.py:34
  48.3 0.7 collective-permute-start.13
  49.0 0.3 collective-permute-done.14.rest_8_.refs_1_.refs_8_
  49.3 0.7 collective-permute-start.12
  49.9 10.6 %collective-permute-done.7.rest_1_ = bf16[128,2048]{1,0:T(8,128)(2,1)S(1)} collective-permute-done((bf16[128,2048]{1,0:T(8,128)(2,1)S(1)}, bf16[128,2048]{1,0:T(8,128)(2,1)S(1)}, u32[]{:S(2)}, u32[]{:S(2)}) %collective-permute-start.7) | collective-permute-done | bytes 524320 | tf_op jit(solution)/shard_map/ppermute | solution.py:34
  60.5 1.3 collective-permute-start.11
  61.8 1.3 norm_forward.6.rest_0_
  63.1 1.5 %norm_forward.7.rest_4_ = bf16[128,2560]{1,0:T(8,128)(2,1)S(1)} custom-call(s32[2]{0:T(128)S(1)} %pad_add_fusion.place_ref, bf16[128,8192]{1,0:T(8,128)(2,1)S(1)} %bitcast.16, bf16[1,8192]{1,0:T(2,128)(2,1)S(1)} %copy-done.5, bf16[128,512]{1,0:T(8,128)(2,1)S(1)} %attend.1.cot_ref, bf16[96,2560]{1,0:T(8,128)(2,1)S(1)} %norm_forward.6.rest_0_), custom_call_target="tpu_custom_call" | custom-call | flops 4194304 | bytes 2752512 | tf_op jit(solution)/shard_map/norm_forward/pallas_call | solution.py:92
  64.6 26.5 %collective-permute-done.8.rest_2_ = bf16[128,2048]{1,0:T(8,128)(2,1)S(1)} collective-permute-done((bf16[128,2048]{1,0:T(8,128)(2,1)S(1)}, bf16[128,2048]{1,0:T(8,128)(2,1)S(1)}, u32[]{:S(2)}, u32[]{:S(2)}) %collective-permute-start.8) | collective-permute-done | bytes 524320 | tf_op jit(solution)/shard_map/ppermute | solution.py:34
  91.1 1.6 %collective-permute-done.9.rest_3_ = bf16[128,2048]{1,0:T(8,128)(2,1)S(1)} collective-permute-done((bf16[128,2048]{1,0:T(8,128)(2,1)S(1)}, bf16[128,2048]{1,0:T(8,128)(2,1)S(1)}, u32[]{:S(2)}, u32[]{:S(2)}) %collective-permute-start.9) | collective-permute-done | bytes 524320 | tf_op jit(solution)/shard_map/ppermute | solution.py:34
  92.7 3.3 %norm_backward.1 = bf16[128,8192]{1,0:T(8,128)(2,1)S(1)} custom-call(s32[2]{0:T(128)S(1)} %pad_add_fusion.place_ref, bf16[128,8192]{1,0:T(8,128)(2,1)S(1)} %bitcast.17, bf16[1,8192]{1,0:T(2,128)(2,1)S(1)} %copy-done.7, bf16[128,8192]{1,0:T(8,128)(2,1)S(1)} %bitcast.18, bf16[128,2048]{1,0:T(8,128)(2,1)S(1)} %get-tuple-element.9.rest_0_, ...), custom_call_target="tpu_custom_call" | custom-call | flops 10485760 | bytes 8388608 | tf_op jit(solution)/shard_map/norm_backward/pallas_call | solution.py:249
  96.0 1.9 %collective-permute-start.15 = (bf16[128,8192]{1,0:T(8,128)(2,1)S(1)}, bf16[128,8192]{1,0:T(8,128)(2,1)S(1)}, u32[]{:S(2)}, u32[]{:S(2)}) collective-permute-start(bf16[128,8192]{1,0:T(8,128)(2,1)S(1)} %norm_backward.1), channel_id=1, source_target_pairs={{8,0},{16,8},{24,16},{9,1},{17,9},{25,17},{10,2},{18,10},{26,18},{... | collective-permute-start | bytes 6291464 | tf_op jit(solution)/shard_map/ppermute | solution.py:25
  97.9 0.1 collective-permute-start.17
  98.0 1.9 %collective-permute-start.16 = (bf16[96,2560]{1,0:T(8,128)(2,1)S(1)}, bf16[96,2560]{1,0:T(8,128)(2,1)S(1)}, u32[]{:S(2)}, u32[]{:S(2)}) collective-permute-start(bf16[96,2560]{1,0:T(8,128)(2,1)S(1)} %norm_forward.6.rest_0_), channel_id=1, source_target_pairs={{0,4},{1,5},{2,6},{3,7},{4,0},{5,1},{6,2},{7,3},{8,12},{9,13},{10,... | collective-permute-start | bytes 1474568 | tf_op jit(solution)/shard_map/ppermute | solution.py:34
  99.8 26.3 %collective-permute-done.17.refs_2_.refs_9_ = bf16[128,2560]{1,0:T(8,128)(2,1)S(1)} collective-permute-done((bf16[128,2560]{1,0:T(8,128)(2,1)S(1)}, bf16[128,2560]{1,0:T(8,128)(2,1)S(1)}, u32[]{:S(2)}, u32[]{:S(2)}) %collective-permute-start.17) | collective-permute-done | bytes 655392 | tf_op jit(solution)/shard_map/ppermute | solution.py:34
  126.1 2.1 %outer.5.refs_2_ = f32[1024,512]{1,0:T(8,128)S(1)} custom-call(bf16[128,2560]{1,0:T(8,128)(2,1)S(1)} %get-tuple-element.8.refs_4_.refs_0_.refs_7_, bf16[128,2560]{1,0:T(8,128)(2,1)S(1)} %collective-permute-done.14.rest_8_.refs_1_.refs_8_, bf16[128,2560]{1,0:T(8,128)(2,1)S(1)} %collective-permute-done.17.refs_2_.refs_9_, ...), custom_call_target="tpu_custom_call" | custom-call | flops 536870912 | bytes 3145728 | tf_op jit(solution)/shard_map/outer/pallas_call | solution.py:290
  128.2 6.3 %collective-permute-done.16.refs_0_.refs_1_ = bf16[96,2560]{1,0:T(8,128)(2,1)S(1)} collective-permute-done((bf16[96,2560]{1,0:T(8,128)(2,1)S(1)}, bf16[96,2560]{1,0:T(8,128)(2,1)S(1)}, u32[]{:S(2)}, u32[]{:S(2)}) %collective-permute-start.16) | collective-permute-done | bytes 491552 | tf_op jit(solution)/shard_map/ppermute | solution.py:34
  134.6 1.1 outer.6
  135.7 0.1 collective-permute-start.18
  135.7 2.1 %outer.4.refs_2_ = f32[1024,512]{1,0:T(8,128)S(1)} custom-call(bf16[128,2560]{1,0:T(8,128)(2,1)S(1)} %get-tuple-element.8.refs_4_.refs_0_.refs_7_, bf16[128,2560]{1,0:T(8,128)(2,1)S(1)} %collective-permute-done.14.rest_8_.refs_1_.refs_8_, bf16[128,2560]{1,0:T(8,128)(2,1)S(1)} %collective-permute-done.17.refs_2_.refs_9_, ...), custom_call_target="tpu_custom_call" | custom-call | flops 536870912 | bytes 3145728 | tf_op jit(solution)/shard_map/outer/pallas_call | solution.py:290
  137.9 0.5 collective-permute-done.18.refs_3_
  138.4 2.4 %outer.7 = f32[1024,512]{1,0:T(8,128)} custom-call(bf16[96,2560]{1,0:T(8,128)(2,1)S(1)} %collective-permute-done.16.refs_0_.refs_1_, bf16[96,2560]{1,0:T(8,128)(2,1)S(1)} %collective-permute-done.16.refs_0_.refs_1_, f32[1024,512]{1,0:T(8,128)S(1)} %outer.4.refs_2_, bf16[1024,512]{1,0:T(8,128)(2,1)S(1)} %collective-permute-done.18.refs_3_), custom_call_target="tpu_custom_call" | custom-call | flops 100663296 | bytes 2293760 | tf_op jit(solution)/shard_map/outer/pallas_call | solution.py:290
  140.8 6.0 %collective-permute-done.15 = bf16[128,8192]{1,0:T(8,128)(2,1)S(1)} collective-permute-done((bf16[128,8192]{1,0:T(8,128)(2,1)S(1)}, bf16[128,8192]{1,0:T(8,128)(2,1)S(1)}, u32[]{:S(2)}, u32[]{:S(2)}) %collective-permute-start.15) | collective-permute-done | bytes 2097184 | tf_op jit(solution)/shard_map/ppermute | solution.py:25
  146.8 1.3 copy.15
  (28 shorter events, 0.2 us)
Async XLA Ops:
  0.6 20.0 %copy-start = (bf16[1,128,8192]{2,1,0:T(8,128)(2,1)S(1)}, bf16[1,128,8192]{2,1,0:T(8,128)(2,1)}, u32[]{:S(2)}) copy-start(bf16[1,128,8192]{2,1,0:T(8,128)(2,1)} %param.11) | copy-start | bytes 6291460
  0.6 20.0 %collective-permute-start = (bf16[1024,1024]{1,0:T(8,128)(2,1)}, bf16[1024,1024]{1,0:T(8,128)(2,1)}, u32[]{:S(2)}, u32[]{:S(2)}) collective-permute-start(bf16[1024,1024]{1,0:T(8,128)(2,1)} %bitcast.23), channel_id=1, source_target_pairs={{0,1},{1,0},{2,3},{3,2},{4,5},{5,4},{6,7},{7,6},{8,9},{9,8},{10,11... | collective-permute-start | bytes 6291464 | tf_op jit(solution)/shard_map/ppermute | solution.py:51
  0.7 22.2 %collective-permute-start.3 = (bf16[128,1024]{1,0:T(8,128)(2,1)}, bf16[128,1024]{1,0:T(8,128)(2,1)S(1)}, u32[]{:S(2)}, u32[]{:S(2)}) collective-permute-start(bf16[128,1024]{1,0:T(8,128)(2,1)} %bitcast.25), channel_id=1, source_target_pairs={{8,10},{9,11},{10,12},{11,13},{12,14},{13,15},{14,8},{15,9},{16,18... | collective-permute-start | bytes 786440 | tf_op jit(solution)/shard_map/ppermute | solution.py:34
  4.3 23.2 %collective-permute-start.2 = (bf16[128,1024]{1,0:T(8,128)(2,1)}, bf16[128,1024]{1,0:T(8,128)(2,1)S(1)}, u32[]{:S(2)}, u32[]{:S(2)}) collective-permute-start(bf16[128,1024]{1,0:T(8,128)(2,1)} %bitcast.26), channel_id=1, source_target_pairs={{8,12},{9,13},{10,14},{11,15},{12,8},{13,9},{14,10},{15,11},{16,20... | collective-permute-start | bytes 786440 | tf_op jit(solution)/shard_map/ppermute | solution.py:34
  7.5 21.8 %collective-permute-start.1 = (bf16[128,1024]{1,0:T(8,128)(2,1)}, bf16[128,1024]{1,0:T(8,128)(2,1)S(1)}, u32[]{:S(2)}, u32[]{:S(2)}) collective-permute-start(bf16[128,1024]{1,0:T(8,128)(2,1)} %bitcast.27), channel_id=1, source_target_pairs={{8,14},{9,15},{10,8},{11,9},{12,10},{13,11},{14,12},{15,13},{16,22... | collective-permute-start | bytes 786440 | tf_op jit(solution)/shard_map/ppermute | solution.py:34
  12.0 1.2 copy-start.3
  13.2 1.2 copy-start.4
  14.5 0.9 copy-start.6
  15.4 0.7 copy-start.8
  16.0 4.6 %copy-start.5 = (bf16[1,8192]{1,0:T(2,128)(2,1)S(1)}, bf16[1,8192]{1,0:T(2,128)(2,1)}, u32[]{:S(2)}) copy-start(bf16[1,8192]{1,0:T(2,128)(2,1)} %gain_ref.8) | copy-start | bytes 49156
  21.4 10.3 %copy-start.9 = (bf16[1,1024,1024]{2,1,0:T(8,128)(2,1)S(1)}, bf16[1,1024,1024]{2,1,0:T(8,128)(2,1)}, u32[]{:S(2)}) copy-start(bf16[1,1024,1024]{2,1,0:T(8,128)(2,1)} %param.21) | copy-start | bytes 6291460
  21.4 10.3 %copy-start.10 = (bf16[1,128,1024]{2,1,0:T(8,128)(2,1)S(1)}, bf16[1,128,1024]{2,1,0:T(8,128)(2,1)}, u32[]{:S(2)}) copy-start(bf16[1,128,1024]{2,1,0:T(8,128)(2,1)} %param.20) | copy-start | bytes 786436
  21.4 9.4 %collective-permute-start.6 = (bf16[32,2560]{1,0:T(8,128)(2,1)S(1)}, bf16[32,2560]{1,0:T(8,128)(2,1)S(1)}, u32[]{:S(2)}, u32[]{:S(2)}) collective-permute-start(bf16[32,2560]{1,0:T(8,128)(2,1)S(1)} %norm_forward.4.refs_0_), channel_id=1, source_target_pairs={{24,0},{25,1},{26,2},{27,3},{28,4},{29,5},{30,6},{31,7}} | collective-permute-start | bytes 491528 | tf_op jit(solution)/shard_map/ppermute | solution.py:40
  22.2 8.6 %collective-permute-start.5 = (bf16[32,2560]{1,0:T(8,128)(2,1)S(1)}, bf16[32,2560]{1,0:T(8,128)(2,1)S(1)}, u32[]{:S(2)}, u32[]{:S(2)}) collective-permute-start(bf16[32,2560]{1,0:T(8,128)(2,1)S(1)} %norm_forward.4.refs_0_), channel_id=1, source_target_pairs={{16,0},{17,1},{18,2},{19,3},{20,4},{21,5},{22,6},{23,7}} | collective-permute-start | bytes 491528 | tf_op jit(solution)/shard_map/ppermute | solution.py:40
  22.9 8.0 %collective-permute-start.4 = (bf16[32,2560]{1,0:T(8,128)(2,1)S(1)}, bf16[32,2560]{1,0:T(8,128)(2,1)S(1)}, u32[]{:S(2)}, u32[]{:S(2)}) collective-permute-start(bf16[32,2560]{1,0:T(8,128)(2,1)S(1)} %norm_forward.4.refs_0_), channel_id=1, source_target_pairs={{8,0},{9,1},{10,2},{11,3},{12,4},{13,5},{14,6},{15,7}} | collective-permute-start | bytes 491528 | tf_op jit(solution)/shard_map/ppermute | solution.py:40
  30.9 17.3 %collective-permute-start.10 = (bf16[128,2560]{1,0:T(8,128)(2,1)S(1)}, bf16[128,2560]{1,0:T(8,128)(2,1)S(1)}, u32[]{:S(2)}, u32[]{:S(2)}) collective-permute-start(bf16[128,2560]{1,0:T(8,128)(2,1)S(1)} %stack_rows.1.rest_4_), channel_id=1, source_target_pairs={{0,4},{1,5},{2,6},{3,7},{4,0},{5,1},{6,2},{7,3}} | collective-permute-start | bytes 1966088 | tf_op jit(solution)/shard_map/ppermute | solution.py:46
  31.6 17.6 %collective-permute-start.14 = (bf16[128,2560]{1,0:T(8,128)(2,1)S(1)}, bf16[128,2560]{1,0:T(8,128)(2,1)S(1)}, u32[]{:S(2)}, u32[]{:S(2)}) collective-permute-start(bf16[128,2560]{1,0:T(8,128)(2,1)S(1)} %get-tuple-element.13), channel_id=1, source_target_pairs={{0,2},{1,3},{2,4},{3,5},{4,6},{5,7},{6,0},{7,1},{8,10},{9,11},{10,... | collective-permute-start | bytes 1966088 | tf_op jit(solution)/shard_map/ppermute | solution.py:34
  38.1 22.4 %collective-permute-start.7 = (bf16[128,2048]{1,0:T(8,128)(2,1)S(1)}, bf16[128,2048]{1,0:T(8,128)(2,1)S(1)}, u32[]{:S(2)}, u32[]{:S(2)}) collective-permute-start(bf16[128,2048]{1,0:T(8,128)(2,1)S(1)} %get-tuple-element.10), channel_id=1, source_target_pairs={{8,10},{9,11},{10,12},{11,13},{12,14},{13,15},{14,8},{15,9},{16,18... | collective-permute-start | bytes 1572872 | tf_op jit(solution)/shard_map/ppermute | solution.py:34
  42.1 49.0 %collective-permute-start.8 = (bf16[128,2048]{1,0:T(8,128)(2,1)S(1)}, bf16[128,2048]{1,0:T(8,128)(2,1)S(1)}, u32[]{:S(2)}, u32[]{:S(2)}) collective-permute-start(bf16[128,2048]{1,0:T(8,128)(2,1)S(1)} %get-tuple-element.11), channel_id=1, source_target_pairs={{8,12},{9,13},{10,14},{11,15},{12,8},{13,9},{14,10},{15,11},{16,20... | collective-permute-start | bytes 1572872 | tf_op jit(solution)/shard_map/ppermute | solution.py:34
  46.3 46.4 %collective-permute-start.9 = (bf16[128,2048]{1,0:T(8,128)(2,1)S(1)}, bf16[128,2048]{1,0:T(8,128)(2,1)S(1)}, u32[]{:S(2)}, u32[]{:S(2)}) collective-permute-start(bf16[128,2048]{1,0:T(8,128)(2,1)S(1)} %get-tuple-element.12), channel_id=1, source_target_pairs={{8,14},{9,15},{10,8},{11,9},{12,10},{13,11},{14,12},{15,13},{16,22... | collective-permute-start | bytes 1572872 | tf_op jit(solution)/shard_map/ppermute | solution.py:34
  48.3 44.4 %collective-permute-start.13 = (bf16[32,2560]{1,0:T(8,128)(2,1)S(1)}, bf16[32,2560]{1,0:T(8,128)(2,1)S(1)}, u32[]{:S(2)}, u32[]{:S(2)}) collective-permute-start(bf16[32,2560]{1,0:T(8,128)(2,1)S(1)} %get-tuple-element.15), channel_id=1, source_target_pairs={{0,24},{1,25},{2,26},{3,27},{4,28},{5,29},{6,30},{7,31}} | collective-permute-start | bytes 491528 | tf_op jit(solution)/shard_map/ppermute | solution.py:40
  49.3 43.4 %collective-permute-start.12 = (bf16[32,2560]{1,0:T(8,128)(2,1)S(1)}, bf16[32,2560]{1,0:T(8,128)(2,1)S(1)}, u32[]{:S(2)}, u32[]{:S(2)}) collective-permute-start(bf16[32,2560]{1,0:T(8,128)(2,1)S(1)} %get-tuple-element.16), channel_id=1, source_target_pairs={{0,16},{1,17},{2,18},{3,19},{4,20},{5,21},{6,22},{7,23}} | collective-permute-start | bytes 491528 | tf_op jit(solution)/shard_map/ppermute | solution.py:40
  60.5 32.2 %collective-permute-start.11 = (bf16[32,2560]{1,0:T(8,128)(2,1)S(1)}, bf16[32,2560]{1,0:T(8,128)(2,1)S(1)}, u32[]{:S(2)}, u32[]{:S(2)}) collective-permute-start(bf16[32,2560]{1,0:T(8,128)(2,1)S(1)} %get-tuple-element.17), channel_id=1, source_target_pairs={{0,8},{1,9},{2,10},{3,11},{4,12},{5,13},{6,14},{7,15}} | collective-permute-start | bytes 491528 | tf_op jit(solution)/shard_map/ppermute | solution.py:40
  61.8 30.9 %copy-start.2 = (bf16[1,128,8192]{2,1,0:T(8,128)(2,1)S(1)}, bf16[1,128,8192]{2,1,0:T(8,128)(2,1)}, u32[]{:S(2)}) copy-start(bf16[1,128,8192]{2,1,0:T(8,128)(2,1)} %param.19) | copy-start | bytes 6291460
  63.1 29.6 %copy-start.1 = (bf16[1,128,8192]{2,1,0:T(8,128)(2,1)S(1)}, bf16[1,128,8192]{2,1,0:T(8,128)(2,1)}, u32[]{:S(2)}) copy-start(bf16[1,128,8192]{2,1,0:T(8,128)(2,1)} %param.17) | copy-start | bytes 6291460
  63.1 29.6 %copy-start.7 = (bf16[1,8192]{1,0:T(2,128)(2,1)S(1)}, bf16[1,8192]{1,0:T(2,128)(2,1)}, u32[]{:S(2)}) copy-start(bf16[1,8192]{1,0:T(2,128)(2,1)} %gain_ref.9) | copy-start | bytes 49156
  96.0 50.8 %collective-permute-start.15 = (bf16[128,8192]{1,0:T(8,128)(2,1)S(1)}, bf16[128,8192]{1,0:T(8,128)(2,1)S(1)}, u32[]{:S(2)}, u32[]{:S(2)}) collective-permute-start(bf16[128,8192]{1,0:T(8,128)(2,1)S(1)} %norm_backward.1), channel_id=1, source_target_pairs={{8,0},{16,8},{24,16},{9,1},{17,9},{25,17},{10,2},{18,10},{26,18},{... | collective-permute-start | bytes 6291464 | tf_op jit(solution)/shard_map/ppermute | solution.py:25
  97.9 28.2 %collective-permute-start.17 = (bf16[128,2560]{1,0:T(8,128)(2,1)S(1)}, bf16[128,2560]{1,0:T(8,128)(2,1)S(1)}, u32[]{:S(2)}, u32[]{:S(2)}) collective-permute-start(bf16[128,2560]{1,0:T(8,128)(2,1)S(1)} %norm_forward.7.rest_4_), channel_id=1, source_target_pairs={{0,6},{1,7},{2,0},{3,1},{4,2},{5,3},{6,4},{7,5},{8,14},{9,15},{10,... | collective-permute-start | bytes 1966088 | tf_op jit(solution)/shard_map/ppermute | solution.py:34
  98.0 36.6 %collective-permute-start.16 = (bf16[96,2560]{1,0:T(8,128)(2,1)S(1)}, bf16[96,2560]{1,0:T(8,128)(2,1)S(1)}, u32[]{:S(2)}, u32[]{:S(2)}) collective-permute-start(bf16[96,2560]{1,0:T(8,128)(2,1)S(1)} %norm_forward.6.rest_0_), channel_id=1, source_target_pairs={{0,4},{1,5},{2,6},{3,7},{4,0},{5,1},{6,2},{7,3},{8,12},{9,13},{10,... | collective-permute-start | bytes 1474568 | tf_op jit(solution)/shard_map/ppermute | solution.py:34
  135.7 2.7 %collective-permute-start.18 = (bf16[1024,512]{1,0:T(8,128)(2,1)S(1)}, bf16[1024,512]{1,0:T(8,128)(2,1)S(1)}, u32[]{:S(2)}, u32[]{:S(2)}) collective-permute-start(bf16[1024,512]{1,0:T(8,128)(2,1)S(1)} %outer.6), channel_id=1, source_target_pairs={{0,1},{1,0},{2,3},{3,2},{4,5},{5,4},{6,7},{7,6},{8,9},{9,8},{10,11... | collective-permute-start | bytes 3145736 | tf_op jit(solution)/shard_map/ppermute | solution.py:51
where the time goes:
time: 149 us; the launch traced here: 148 us
  waiting for transfers between devices  83.2 us (56%)
  starting transfers between devices  30.7 us (21%)
  Pallas kernels  27 us (18%)
  local copies, waits for them, and re-layouts  6.17 us (4%)
    ppermute x9, waiting for transfers between devices, along_chips(): return lax.ppermute(array, ('pipe', 'dp'), pairs)  76.6 us
    ppermute x9, starting transfers between devices, along_chips(): return lax.ppermute(array, ('pipe', 'dp'), pairs)  22.5 us
    pallas_call x4, Pallas kernels, outer(): call(functools.partial(outer_kernel, [len(group) for group in groups], le...  7.73 us
    pallas_call x1, Pallas kernels, project(): call(functools.partial(project_kernel, chips, steps), 'project', 4 * chip...  6.39 us
    ppermute x1, waiting for transfers between devices, from_behind(): return lax.ppermute(array, axis, pairs)  6.03 us
    ppermute x6, starting transfers between devices, between_lines(): return lax.ppermute(array, ('pipe', 'dp'), pairs)  5.38 us
    unnamed x23, local copies, waits for them, and re-layouts  5.36 us
    pallas_call x4, Pallas kernels, normalize(): call(functools.partial(norm_kernel, chips, ahead), 'norm_forward', 4 * co...  5.07 us
  transfers between devices with their start and end apart: 19, of which 10 were waited for; matrix products, arithmetic and copies ran while one was open for 1% of the time, Pallas kernels for 16%

commit v1 on v0

--- a/solution.py
+++ b/solution.py
@@ -28,8 +28,8 @@
 def along_chips(array, by, first=0):
     length = lax.axis_size("dp")
     pairs = [
-        (line * length + i, line * length + (i + by * CORES) % length)
-        for line in range(first, lax.axis_size("pipe")) for i in range(length)
+        (line * length + i, line * length + ((i + by * CORES) % length if line >= first else i ^ 1))
+        for line in range(lax.axis_size("pipe")) for i in range(length)
     ]
     return lax.ppermute(array, ("pipe", "dp"), pairs)
 
@@ -199,7 +199,7 @@
     chips = len(rows)
     taken, depth = rows[0].shape
     width = own.shape[0]
-    block = min(width, 256)
+    block = min(width, 512)
     steps = width // block
     return call(
         functools.partial(project_kernel, chips, steps), "project",

time: 149 us -> 146 us (0.980)
  starting transfers between devices: 30.7 us -> 19.1 us
  waiting for transfers between devices: 83.2 us -> 94 us
    ppermute x9, starting transfers between devices: 22.5 us -> 10.9 us  [along_chips(): return lax.ppermute(array, ('pipe', 'dp'), pairs)]
    ppermute x9, waiting for transfers between devices: 76.6 us -> 87.9 us  [along_chips(): return lax.ppermute(array, ('pipe', 'dp'), pairs)]
  transfers between devices with their start and end apart: 19 -> 19, of which waited for: 10 -> 11; matrix products, arithmetic and copies ran while one was open for 1% -> 1% of each run, Pallas kernels for 16% -> 15%
where the time goes in v1:
time: 146 us
  waiting for transfers between devices  94 us (64%)
  Pallas kernels  25.6 us (18%)
  starting transfers between devices  19.1 us (13%)
  local copies, waits for them, and re-layouts  6.16 us (4%)
    ppermute x9, waiting for transfers between devices, along_chips(): return lax.ppermute(array, ('pipe', 'dp'), pairs)  87.9 us
    ppermute x9, starting transfers between devices, along_chips(): return lax.ppermute(array, ('pipe', 'dp'), pairs)  10.9 us
    pallas_call x4, Pallas kernels, outer(): call(functools.partial(outer_kernel, [len(group) for group in groups], le...  7.75 us
    ppermute x1, waiting for transfers between devices, from_behind(): return lax.ppermute(array, axis, pairs)  5.65 us
    ppermute x6, starting transfers between devices, between_lines(): return lax.ppermute(array, ('pipe', 'dp'), pairs)  5.37 us
    unnamed x23, local copies, waits for them, and re-layouts  5.36 us
    pallas_call x4, Pallas kernels, normalize(): call(functools.partial(norm_kernel, chips, ahead), 'norm_forward', 4 * co...  5.07 us
    pallas_call x1, Pallas kernels, project(): call(functools.partial(project_kernel, chips, steps), 'project', 4 * chip...  4.96 us
  transfers between devices with their start and end apart: 19, of which 11 were waited for; matrix products, arithmetic and copies ran while one was open for 1% of the time, Pallas kernels for 15%

profile of v1, /device:TPU:10, one launch (start us, length us, event | category | flops | bytes accessed | tf_op | source)
XLA Modules:
  0.0 145.9 jit_solution(8618844000355248036)
XLA Ops:
  0.6 0.1 collective-permute-start
  0.7 1.6 %collective-permute-start.3 = (bf16[128,1024]{1,0:T(8,128)(2,1)}, bf16[128,1024]{1,0:T(8,128)(2,1)S(1)}, u32[]{:S(2)}, u32[]{:S(2)}) collective-permute-start(bf16[128,1024]{1,0:T(8,128)(2,1)} %bitcast.25), channel_id=1, source_target_pairs={{0,1},{1,0},{2,3},{3,2},{4,5},{5,4},{6,7},{7,6},{8,10},{9,11},{10,... | collective-permute-start | bytes 786440 | tf_op jit(solution)/shard_map/ppermute | solution.py:34
  2.3 1.2 collective-permute-start.2
  3.6 1.8 %collective-permute-start.1 = (bf16[128,1024]{1,0:T(8,128)(2,1)}, bf16[128,1024]{1,0:T(8,128)(2,1)S(1)}, u32[]{:S(2)}, u32[]{:S(2)}) collective-permute-start(bf16[128,1024]{1,0:T(8,128)(2,1)} %bitcast.27), channel_id=1, source_target_pairs={{0,1},{1,0},{2,3},{3,2},{4,5},{5,4},{6,7},{7,6},{8,14},{9,15},{10,... | collective-permute-start | bytes 786440 | tf_op jit(solution)/shard_map/ppermute | solution.py:34
  5.4 0.8 copy.13.col_seg_ref
  6.2 1.2 copy-done.3
  7.4 1.2 copy-done.4
  8.6 0.9 copy-done.6
  9.5 0.7 copy-done.8
  10.2 4.5 %attend.1.cot_ref = bf16[128,512]{1,0:T(8,128)(2,1)S(1)} custom-call(bf16[128,4096]{1,0:T(8,128)(2,1)S(1)} %bitcast.19, bf16[128,512]{1,0:T(8,128)(2,1)S(1)} %bitcast.21, bf16[128,4096]{1,0:T(8,128)(2,1)S(1)} %bitcast.20, s32[1,128]{1,0:T(1,128)S(1)} %copy-done.8, s32[128,1]{1,0:T(8,128)S(1)} %copy.13.col_seg_ref), custom_call_target="tpu_custom_call" | custom-call | flops 268435456 | bytes 2097152 | tf_op jit(solution)/shard_map/attend/pallas_call | solution.py:155
  14.7 0.1 pad_add_fusion.place_ref
  14.7 0.8 norm_forward.4.refs_0_
  15.5 0.0 copy-start.10
  15.5 0.8 collective-permute-start.6
  16.3 0.7 collective-permute-start.5
  17.0 3.4 %collective-permute-done.3.rest_2_.rest_3_ = bf16[128,1024]{1,0:T(8,128)(2,1)S(1)} collective-permute-done((bf16[128,1024]{1,0:T(8,128)(2,1)}, bf16[128,1024]{1,0:T(8,128)(2,1)S(1)}, u32[]{:S(2)}, u32[]{:S(2)}) %collective-permute-start.3) | collective-permute-done | bytes 262176 | tf_op jit(solution)/shard_map/ppermute | solution.py:34
  20.4 1.3 collective-permute-start.4
  21.7 4.0 %collective-permute-done.2.rest_1_.rest_2_ = bf16[128,1024]{1,0:T(8,128)(2,1)S(1)} collective-permute-done((bf16[128,1024]{1,0:T(8,128)(2,1)}, bf16[128,1024]{1,0:T(8,128)(2,1)S(1)}, u32[]{:S(2)}, u32[]{:S(2)}) %collective-permute-start.2) | collective-permute-done | bytes 262176 | tf_op jit(solution)/shard_map/ppermute | solution.py:34
  25.7 1.7 %collective-permute-done.1.rest_0_.rest_1_ = bf16[128,1024]{1,0:T(8,128)(2,1)S(1)} collective-permute-done((bf16[128,1024]{1,0:T(8,128)(2,1)}, bf16[128,1024]{1,0:T(8,128)(2,1)S(1)}, u32[]{:S(2)}, u32[]{:S(2)}) %collective-permute-start.1) | collective-permute-done | bytes 262176 | tf_op jit(solution)/shard_map/ppermute | solution.py:34
  27.4 1.5 %norm_forward.5 = (bf16[128,2560]{1,0:T(8,128)(2,1)S(1)}, bf16[128,2560]{1,0:T(8,128)(2,1)S(1)}) custom-call(s32[2]{0:T(128)S(1)} %pad_add_fusion.place_ref, bf16[128,8192]{1,0:T(8,128)(2,1)S(1)} %bitcast.14, bf16[1,8192]{1,0:T(2,128)(2,1)S(1)} %copy-done.5, bf16[128,512]{1,0:T(8,128)(2,1)S(1)} %attend.1.cot_ref, ...), custom_call_target="tpu_custom_call" | custom-call | flops 4194304 | bytes 3407872 | tf_op jit(solution)/shard_map/norm_forward/pallas_call | solution.py:92
  29.0 0.7 collective-permute-start.10
  29.7 0.1 collective-permute-start.14
  29.8 5.0 %project.1 = (bf16[128,2048]{1,0:T(8,128)(2,1)S(1)}, bf16[128,2048]{1,0:T(8,128)(2,1)S(1)}, bf16[128,2048]{1,0:T(8,128)(2,1)S(1)}, bf16[128,2048]{1,0:T(8,128)(2,1)S(1)}) custom-call(bf16[1024,1024]{1,0:T(8,128)(2,1)S(1)} %bitcast.24, bf16[1024,1024]{1,0:T(8,128)(2,1)} %collective-permute-done.rest_0_.other_ref, bf16[128,1024]{1,0:T(8,128)(2,1)S(1)} %bitcast.28, ...), custom_call_target="tpu_custom_call" | custom-call | flops 2147483648 | bytes 7340032 | tf_op jit(solution)/shard_map/project/pallas_call | solution.py:204
  34.8 2.2 %collective-permute-start.7 = (bf16[128,2048]{1,0:T(8,128)(2,1)S(1)}, bf16[128,2048]{1,0:T(8,128)(2,1)S(1)}, u32[]{:S(2)}, u32[]{:S(2)}) collective-permute-start(bf16[128,2048]{1,0:T(8,128)(2,1)S(1)} %get-tuple-element.10), channel_id=1, source_target_pairs={{0,1},{1,0},{2,3},{3,2},{4,5},{5,4},{6,7},{7,6},{8,10},{9,11},{10,... | collective-permute-start | bytes 1572872 | tf_op jit(solution)/shard_map/ppermute | solution.py:34
  36.9 2.2 %collective-permute-start.8 = (bf16[128,2048]{1,0:T(8,128)(2,1)S(1)}, bf16[128,2048]{1,0:T(8,128)(2,1)S(1)}, u32[]{:S(2)}, u32[]{:S(2)}) collective-permute-start(bf16[128,2048]{1,0:T(8,128)(2,1)S(1)} %get-tuple-element.11), channel_id=1, source_target_pairs={{0,1},{1,0},{2,3},{3,2},{4,5},{5,4},{6,7},{7,6},{8,12},{9,13},{10,... | collective-permute-start | bytes 1572872 | tf_op jit(solution)/shard_map/ppermute | solution.py:34
  39.2 0.7 collective-permute-start.13
  39.9 7.5 %collective-permute-done.14.rest_8_.refs_1_.refs_8_ = bf16[128,2560]{1,0:T(8,128)(2,1)S(1)} collective-permute-done((bf16[128,2560]{1,0:T(8,128)(2,1)S(1)}, bf16[128,2560]{1,0:T(8,128)(2,1)S(1)}, u32[]{:S(2)}, u32[]{:S(2)}) %collective-permute-start.14) | collective-permute-done | bytes 655392 | tf_op jit(solution)/shard_map/ppermute | solution.py:34
  47.4 0.7 collective-permute-start.12
  48.0 10.6 %collective-permute-done.7.rest_1_ = bf16[128,2048]{1,0:T(8,128)(2,1)S(1)} collective-permute-done((bf16[128,2048]{1,0:T(8,128)(2,1)S(1)}, bf16[128,2048]{1,0:T(8,128)(2,1)S(1)}, u32[]{:S(2)}, u32[]{:S(2)}) %collective-permute-start.7) | collective-permute-done | bytes 524320 | tf_op jit(solution)/shard_map/ppermute | solution.py:34
  58.6 1.3 collective-permute-start.11
  59.9 1.3 norm_forward.6.rest_0_
  61.2 1.5 %norm_forward.7.rest_4_ = bf16[128,2560]{1,0:T(8,128)(2,1)S(1)} custom-call(s32[2]{0:T(128)S(1)} %pad_add_fusion.place_ref, bf16[128,8192]{1,0:T(8,128)(2,1)S(1)} %bitcast.16, bf16[1,8192]{1,0:T(2,128)(2,1)S(1)} %copy-done.5, bf16[128,512]{1,0:T(8,128)(2,1)S(1)} %attend.1.cot_ref, bf16[96,2560]{1,0:T(8,128)(2,1)S(1)} %norm_forward.6.rest_0_), custom_call_target="tpu_custom_call" | custom-call | flops 4194304 | bytes 2752512 | tf_op jit(solution)/shard_map/norm_forward/pallas_call | solution.py:92
  62.7 26.5 %collective-permute-done.8.rest_2_ = bf16[128,2048]{1,0:T(8,128)(2,1)S(1)} collective-permute-done((bf16[128,2048]{1,0:T(8,128)(2,1)S(1)}, bf16[128,2048]{1,0:T(8,128)(2,1)S(1)}, u32[]{:S(2)}, u32[]{:S(2)}) %collective-permute-start.8) | collective-permute-done | bytes 524320 | tf_op jit(solution)/shard_map/ppermute | solution.py:34
  89.2 1.7 %collective-permute-done.9.rest_3_ = bf16[128,2048]{1,0:T(8,128)(2,1)S(1)} collective-permute-done((bf16[128,2048]{1,0:T(8,128)(2,1)S(1)}, bf16[128,2048]{1,0:T(8,128)(2,1)S(1)}, u32[]{:S(2)}, u32[]{:S(2)}) %collective-permute-start.9) | collective-permute-done | bytes 524320 | tf_op jit(solution)/shard_map/ppermute | solution.py:34
  90.9 3.3 %norm_backward.1 = bf16[128,8192]{1,0:T(8,128)(2,1)S(1)} custom-call(s32[2]{0:T(128)S(1)} %pad_add_fusion.place_ref, bf16[128,8192]{1,0:T(8,128)(2,1)S(1)} %bitcast.17, bf16[1,8192]{1,0:T(2,128)(2,1)S(1)} %copy-done.7, bf16[128,8192]{1,0:T(8,128)(2,1)S(1)} %bitcast.18, bf16[128,2048]{1,0:T(8,128)(2,1)S(1)} %get-tuple-element.9.rest_0_, ...), custom_call_target="tpu_custom_call" | custom-call | flops 10485760 | bytes 8388608 | tf_op jit(solution)/shard_map/norm_backward/pallas_call | solution.py:249
  94.2 1.9 %collective-permute-start.15 = (bf16[128,8192]{1,0:T(8,128)(2,1)S(1)}, bf16[128,8192]{1,0:T(8,128)(2,1)S(1)}, u32[]{:S(2)}, u32[]{:S(2)}) collective-permute-start(bf16[128,8192]{1,0:T(8,128)(2,1)S(1)} %norm_backward.1), channel_id=1, source_target_pairs={{8,0},{16,8},{24,16},{9,1},{17,9},{25,17},{10,2},{18,10},{26,18},{... | collective-permute-start | bytes 6291464 | tf_op jit(solution)/shard_map/ppermute | solution.py:25
  96.1 0.1 collective-permute-start.17
  96.2 1.8 %collective-permute-start.16 = (bf16[96,2560]{1,0:T(8,128)(2,1)S(1)}, bf16[96,2560]{1,0:T(8,128)(2,1)S(1)}, u32[]{:S(2)}, u32[]{:S(2)}) collective-permute-start(bf16[96,2560]{1,0:T(8,128)(2,1)S(1)} %norm_forward.6.rest_0_), channel_id=1, source_target_pairs={{0,4},{1,5},{2,6},{3,7},{4,0},{5,1},{6,2},{7,3},{8,12},{9,13},{10,... | collective-permute-start | bytes 1474568 | tf_op jit(solution)/shard_map/ppermute | solution.py:34
  98.0 26.4 %collective-permute-done.17.refs_2_.refs_9_ = bf16[128,2560]{1,0:T(8,128)(2,1)S(1)} collective-permute-done((bf16[128,2560]{1,0:T(8,128)(2,1)S(1)}, bf16[128,2560]{1,0:T(8,128)(2,1)S(1)}, u32[]{:S(2)}, u32[]{:S(2)}) %collective-permute-start.17) | collective-permute-done | bytes 655392 | tf_op jit(solution)/shard_map/ppermute | solution.py:34
  124.3 2.1 %outer.5.refs_2_ = f32[1024,512]{1,0:T(8,128)S(1)} custom-call(bf16[128,2560]{1,0:T(8,128)(2,1)S(1)} %get-tuple-element.8.refs_4_.refs_0_.refs_7_, bf16[128,2560]{1,0:T(8,128)(2,1)S(1)} %collective-permute-done.14.rest_8_.refs_1_.refs_8_, bf16[128,2560]{1,0:T(8,128)(2,1)S(1)} %collective-permute-done.17.refs_2_.refs_9_, ...), custom_call_target="tpu_custom_call" | custom-call | flops 536870912 | bytes 3145728 | tf_op jit(solution)/shard_map/outer/pallas_call | solution.py:290
  126.5 6.2 %collective-permute-done.16.refs_0_.refs_1_ = bf16[96,2560]{1,0:T(8,128)(2,1)S(1)} collective-permute-done((bf16[96,2560]{1,0:T(8,128)(2,1)S(1)}, bf16[96,2560]{1,0:T(8,128)(2,1)S(1)}, u32[]{:S(2)}, u32[]{:S(2)}) %collective-permute-start.16) | collective-permute-done | bytes 491552 | tf_op jit(solution)/shard_map/ppermute | solution.py:34
  132.7 1.1 outer.6
  133.8 0.1 collective-permute-start.18
  133.9 2.1 %outer.4.refs_2_ = f32[1024,512]{1,0:T(8,128)S(1)} custom-call(bf16[128,2560]{1,0:T(8,128)(2,1)S(1)} %get-tuple-element.8.refs_4_.refs_0_.refs_7_, bf16[128,2560]{1,0:T(8,128)(2,1)S(1)} %collective-permute-done.14.rest_8_.refs_1_.refs_8_, bf16[128,2560]{1,0:T(8,128)(2,1)S(1)} %collective-permute-done.17.refs_2_.refs_9_, ...), custom_call_target="tpu_custom_call" | custom-call | flops 536870912 | bytes 3145728 | tf_op jit(solution)/shard_map/outer/pallas_call | solution.py:290
  136.0 0.5 collective-permute-done.18.refs_3_
  136.5 2.4 %outer.7 = f32[1024,512]{1,0:T(8,128)} custom-call(bf16[96,2560]{1,0:T(8,128)(2,1)S(1)} %collective-permute-done.16.refs_0_.refs_1_, bf16[96,2560]{1,0:T(8,128)(2,1)S(1)} %collective-permute-done.16.refs_0_.refs_1_, f32[1024,512]{1,0:T(8,128)S(1)} %outer.4.refs_2_, bf16[1024,512]{1,0:T(8,128)(2,1)S(1)} %collective-permute-done.18.refs_3_), custom_call_target="tpu_custom_call" | custom-call | flops 100663296 | bytes 2293760 | tf_op jit(solution)/shard_map/outer/pallas_call | solution.py:290
  138.9 5.6 %collective-permute-done.15 = bf16[128,8192]{1,0:T(8,128)(2,1)S(1)} collective-permute-done((bf16[128,8192]{1,0:T(8,128)(2,1)S(1)}, bf16[128,8192]{1,0:T(8,128)(2,1)S(1)}, u32[]{:S(2)}, u32[]{:S(2)}) %collective-permute-start.15) | collective-permute-done | bytes 2097184 | tf_op jit(solution)/shard_map/ppermute | solution.py:25
  144.6 1.3 copy.15
  (28 shorter events, 0.2 us)
Async XLA Ops:
  0.6 14.1 %copy-start = (bf16[1,128,8192]{2,1,0:T(8,128)(2,1)S(1)}, bf16[1,128,8192]{2,1,0:T(8,128)(2,1)}, u32[]{:S(2)}) copy-start(bf16[1,128,8192]{2,1,0:T(8,128)(2,1)} %param.11) | copy-start | bytes 6291460
  0.6 14.1 %collective-permute-start = (bf16[1024,1024]{1,0:T(8,128)(2,1)}, bf16[1024,1024]{1,0:T(8,128)(2,1)}, u32[]{:S(2)}, u32[]{:S(2)}) collective-permute-start(bf16[1024,1024]{1,0:T(8,128)(2,1)} %bitcast.23), channel_id=1, source_target_pairs={{0,1},{1,0},{2,3},{3,2},{4,5},{5,4},{6,7},{7,6},{8,9},{9,8},{10,11... | collective-permute-start | bytes 6291464 | tf_op jit(solution)/shard_map/ppermute | solution.py:51
  0.7 19.7 %collective-permute-start.3 = (bf16[128,1024]{1,0:T(8,128)(2,1)}, bf16[128,1024]{1,0:T(8,128)(2,1)S(1)}, u32[]{:S(2)}, u32[]{:S(2)}) collective-permute-start(bf16[128,1024]{1,0:T(8,128)(2,1)} %bitcast.25), channel_id=1, source_target_pairs={{0,1},{1,0},{2,3},{3,2},{4,5},{5,4},{6,7},{7,6},{8,10},{9,11},{10,... | collective-permute-start | bytes 786440 | tf_op jit(solution)/shard_map/ppermute | solution.py:34
  2.3 23.3 %collective-permute-start.2 = (bf16[128,1024]{1,0:T(8,128)(2,1)}, bf16[128,1024]{1,0:T(8,128)(2,1)S(1)}, u32[]{:S(2)}, u32[]{:S(2)}) collective-permute-start(bf16[128,1024]{1,0:T(8,128)(2,1)} %bitcast.26), channel_id=1, source_target_pairs={{0,1},{1,0},{2,3},{3,2},{4,5},{5,4},{6,7},{7,6},{8,12},{9,13},{10,... | collective-permute-start | bytes 786440 | tf_op jit(solution)/shard_map/ppermute | solution.py:34
  3.6 23.8 %collective-permute-start.1 = (bf16[128,1024]{1,0:T(8,128)(2,1)}, bf16[128,1024]{1,0:T(8,128)(2,1)S(1)}, u32[]{:S(2)}, u32[]{:S(2)}) collective-permute-start(bf16[128,1024]{1,0:T(8,128)(2,1)} %bitcast.27), channel_id=1, source_target_pairs={{0,1},{1,0},{2,3},{3,2},{4,5},{5,4},{6,7},{7,6},{8,14},{9,15},{10,... | collective-permute-start | bytes 786440 | tf_op jit(solution)/shard_map/ppermute | solution.py:34
  6.2 1.2 copy-start.3
  7.4 1.2 copy-start.4
  8.6 0.9 copy-start.6
  9.5 0.7 copy-start.8
  10.2 4.6 %copy-start.5 = (bf16[1,8192]{1,0:T(2,128)(2,1)S(1)}, bf16[1,8192]{1,0:T(2,128)(2,1)}, u32[]{:S(2)}) copy-start(bf16[1,8192]{1,0:T(2,128)(2,1)} %gain_ref.8) | copy-start | bytes 49156
  15.5 14.3 %copy-start.9 = (bf16[1,1024,1024]{2,1,0:T(8,128)(2,1)S(1)}, bf16[1,1024,1024]{2,1,0:T(8,128)(2,1)}, u32[]{:S(2)}) copy-start(bf16[1,1024,1024]{2,1,0:T(8,128)(2,1)} %param.21) | copy-start | bytes 6291460
  15.5 14.3 %copy-start.10 = (bf16[1,128,1024]{2,1,0:T(8,128)(2,1)S(1)}, bf16[1,128,1024]{2,1,0:T(8,128)(2,1)}, u32[]{:S(2)}) copy-start(bf16[1,128,1024]{2,1,0:T(8,128)(2,1)} %param.20) | copy-start | bytes 786436
  15.5 13.4 %collective-permute-start.6 = (bf16[32,2560]{1,0:T(8,128)(2,1)S(1)}, bf16[32,2560]{1,0:T(8,128)(2,1)S(1)}, u32[]{:S(2)}, u32[]{:S(2)}) collective-permute-start(bf16[32,2560]{1,0:T(8,128)(2,1)S(1)} %norm_forward.4.refs_0_), channel_id=1, source_target_pairs={{24,0},{25,1},{26,2},{27,3},{28,4},{29,5},{30,6},{31,7}} | collective-permute-start | bytes 491528 | tf_op jit(solution)/shard_map/ppermute | solution.py:40
  16.3 12.6 %collective-permute-start.5 = (bf16[32,2560]{1,0:T(8,128)(2,1)S(1)}, bf16[32,2560]{1,0:T(8,128)(2,1)S(1)}, u32[]{:S(2)}, u32[]{:S(2)}) collective-permute-start(bf16[32,2560]{1,0:T(8,128)(2,1)S(1)} %norm_forward.4.refs_0_), channel_id=1, source_target_pairs={{16,0},{17,1},{18,2},{19,3},{20,4},{21,5},{22,6},{23,7}} | collective-permute-start | bytes 491528 | tf_op jit(solution)/shard_map/ppermute | solution.py:40
  20.4 8.6 %collective-permute-start.4 = (bf16[32,2560]{1,0:T(8,128)(2,1)S(1)}, bf16[32,2560]{1,0:T(8,128)(2,1)S(1)}, u32[]{:S(2)}, u32[]{:S(2)}) collective-permute-start(bf16[32,2560]{1,0:T(8,128)(2,1)S(1)} %norm_forward.4.refs_0_), channel_id=1, source_target_pairs={{8,0},{9,1},{10,2},{11,3},{12,4},{13,5},{14,6},{15,7}} | collective-permute-start | bytes 491528 | tf_op jit(solution)/shard_map/ppermute | solution.py:40
  29.0 10.2 %collective-permute-start.10 = (bf16[128,2560]{1,0:T(8,128)(2,1)S(1)}, bf16[128,2560]{1,0:T(8,128)(2,1)S(1)}, u32[]{:S(2)}, u32[]{:S(2)}) collective-permute-start(bf16[128,2560]{1,0:T(8,128)(2,1)S(1)} %stack_rows.1.rest_4_), channel_id=1, source_target_pairs={{0,4},{1,5},{2,6},{3,7},{4,0},{5,1},{6,2},{7,3}} | collective-permute-start | bytes 1966088 | tf_op jit(solution)/shard_map/ppermute | solution.py:46
  29.7 17.6 %collective-permute-start.14 = (bf16[128,2560]{1,0:T(8,128)(2,1)S(1)}, bf16[128,2560]{1,0:T(8,128)(2,1)S(1)}, u32[]{:S(2)}, u32[]{:S(2)}) collective-permute-start(bf16[128,2560]{1,0:T(8,128)(2,1)S(1)} %get-tuple-element.13), channel_id=1, source_target_pairs={{0,2},{1,3},{2,4},{3,5},{4,6},{5,7},{6,0},{7,1},{8,10},{9,11},{10,... | collective-permute-start | bytes 1966088 | tf_op jit(solution)/shard_map/ppermute | solution.py:34
  34.8 23.8 %collective-permute-start.7 = (bf16[128,2048]{1,0:T(8,128)(2,1)S(1)}, bf16[128,2048]{1,0:T(8,128)(2,1)S(1)}, u32[]{:S(2)}, u32[]{:S(2)}) collective-permute-start(bf16[128,2048]{1,0:T(8,128)(2,1)S(1)} %get-tuple-element.10), channel_id=1, source_target_pairs={{0,1},{1,0},{2,3},{3,2},{4,5},{5,4},{6,7},{7,6},{8,10},{9,11},{10,... | collective-permute-start | bytes 1572872 | tf_op jit(solution)/shard_map/ppermute | solution.py:34
  36.9 52.3 %collective-permute-start.8 = (bf16[128,2048]{1,0:T(8,128)(2,1)S(1)}, bf16[128,2048]{1,0:T(8,128)(2,1)S(1)}, u32[]{:S(2)}, u32[]{:S(2)}) collective-permute-start(bf16[128,2048]{1,0:T(8,128)(2,1)S(1)} %get-tuple-element.11), channel_id=1, source_target_pairs={{0,1},{1,0},{2,3},{3,2},{4,5},{5,4},{6,7},{7,6},{8,12},{9,13},{10,... | collective-permute-start | bytes 1572872 | tf_op jit(solution)/shard_map/ppermute | solution.py:34
  39.2 51.7 %collective-permute-start.9 = (bf16[128,2048]{1,0:T(8,128)(2,1)S(1)}, bf16[128,2048]{1,0:T(8,128)(2,1)S(1)}, u32[]{:S(2)}, u32[]{:S(2)}) collective-permute-start(bf16[128,2048]{1,0:T(8,128)(2,1)S(1)} %get-tuple-element.12), channel_id=1, source_target_pairs={{0,1},{1,0},{2,3},{3,2},{4,5},{5,4},{6,7},{7,6},{8,14},{9,15},{10,... | collective-permute-start | bytes 1572872 | tf_op jit(solution)/shard_map/ppermute | solution.py:34
  39.2 51.7 %collective-permute-start.13 = (bf16[32,2560]{1,0:T(8,128)(2,1)S(1)}, bf16[32,2560]{1,0:T(8,128)(2,1)S(1)}, u32[]{:S(2)}, u32[]{:S(2)}) collective-permute-start(bf16[32,2560]{1,0:T(8,128)(2,1)S(1)} %get-tuple-element.15), channel_id=1, source_target_pairs={{0,24},{1,25},{2,26},{3,27},{4,28},{5,29},{6,30},{7,31}} | collective-permute-start | bytes 491528 | tf_op jit(solution)/shard_map/ppermute | solution.py:40
  47.4 43.5 %collective-permute-start.12 = (bf16[32,2560]{1,0:T(8,128)(2,1)S(1)}, bf16[32,2560]{1,0:T(8,128)(2,1)S(1)}, u32[]{:S(2)}, u32[]{:S(2)}) collective-permute-start(bf16[32,2560]{1,0:T(8,128)(2,1)S(1)} %get-tuple-element.16), channel_id=1, source_target_pairs={{0,16},{1,17},{2,18},{3,19},{4,20},{5,21},{6,22},{7,23}} | collective-permute-start | bytes 491528 | tf_op jit(solution)/shard_map/ppermute | solution.py:40
  58.6 32.3 %collective-permute-start.11 = (bf16[32,2560]{1,0:T(8,128)(2,1)S(1)}, bf16[32,2560]{1,0:T(8,128)(2,1)S(1)}, u32[]{:S(2)}, u32[]{:S(2)}) collective-permute-start(bf16[32,2560]{1,0:T(8,128)(2,1)S(1)} %get-tuple-element.17), channel_id=1, source_target_pairs={{0,8},{1,9},{2,10},{3,11},{4,12},{5,13},{6,14},{7,15}} | collective-permute-start | bytes 491528 | tf_op jit(solution)/shard_map/ppermute | solution.py:40
  59.9 31.0 %copy-start.2 = (bf16[1,128,8192]{2,1,0:T(8,128)(2,1)S(1)}, bf16[1,128,8192]{2,1,0:T(8,128)(2,1)}, u32[]{:S(2)}) copy-start(bf16[1,128,8192]{2,1,0:T(8,128)(2,1)} %param.19) | copy-start | bytes 6291460
  61.2 29.7 %copy-start.1 = (bf16[1,128,8192]{2,1,0:T(8,128)(2,1)S(1)}, bf16[1,128,8192]{2,1,0:T(8,128)(2,1)}, u32[]{:S(2)}) copy-start(bf16[1,128,8192]{2,1,0:T(8,128)(2,1)} %param.17) | copy-start | bytes 6291460
  61.2 29.7 %copy-start.7 = (bf16[1,8192]{1,0:T(2,128)(2,1)S(1)}, bf16[1,8192]{1,0:T(2,128)(2,1)}, u32[]{:S(2)}) copy-start(bf16[1,8192]{1,0:T(2,128)(2,1)} %gain_ref.9) | copy-start | bytes 49156
  94.2 50.3 %collective-permute-start.15 = (bf16[128,8192]{1,0:T(8,128)(2,1)S(1)}, bf16[128,8192]{1,0:T(8,128)(2,1)S(1)}, u32[]{:S(2)}, u32[]{:S(2)}) collective-permute-start(bf16[128,8192]{1,0:T(8,128)(2,1)S(1)} %norm_backward.1), channel_id=1, source_target_pairs={{8,0},{16,8},{24,16},{9,1},{17,9},{25,17},{10,2},{18,10},{26,18},{... | collective-permute-start | bytes 6291464 | tf_op jit(solution)/shard_map/ppermute | solution.py:25
  96.1 28.2 %collective-permute-start.17 = (bf16[128,2560]{1,0:T(8,128)(2,1)S(1)}, bf16[128,2560]{1,0:T(8,128)(2,1)S(1)}, u32[]{:S(2)}, u32[]{:S(2)}) collective-permute-start(bf16[128,2560]{1,0:T(8,128)(2,1)S(1)} %norm_forward.7.rest_4_), channel_id=1, source_target_pairs={{0,6},{1,7},{2,0},{3,1},{4,2},{5,3},{6,4},{7,5},{8,14},{9,15},{10,... | collective-permute-start | bytes 1966088 | tf_op jit(solution)/shard_map/ppermute | solution.py:34
  96.2 36.5 %collective-permute-start.16 = (bf16[96,2560]{1,0:T(8,128)(2,1)S(1)}, bf16[96,2560]{1,0:T(8,128)(2,1)S(1)}, u32[]{:S(2)}, u32[]{:S(2)}) collective-permute-start(bf16[96,2560]{1,0:T(8,128)(2,1)S(1)} %norm_forward.6.rest_0_), channel_id=1, source_target_pairs={{0,4},{1,5},{2,6},{3,7},{4,0},{5,1},{6,2},{7,3},{8,12},{9,13},{10,... | collective-permute-start | bytes 1474568 | tf_op jit(solution)/shard_map/ppermute | solution.py:34
  133.8 2.7 %collective-permute-start.18 = (bf16[1024,512]{1,0:T(8,128)(2,1)S(1)}, bf16[1024,512]{1,0:T(8,128)(2,1)S(1)}, u32[]{:S(2)}, u32[]{:S(2)}) collective-permute-start(bf16[1024,512]{1,0:T(8,128)(2,1)S(1)} %outer.6), channel_id=1, source_target_pairs={{0,1},{1,0},{2,3},{3,2},{4,5},{5,4},{6,7},{7,6},{8,9},{9,8},{10,11... | collective-permute-start | bytes 3145736 | tf_op jit(solution)/shard_map/ppermute | solution.py:51

commit v2 on v1

--- a/solution.py
+++ b/solution.py
@@ -168,8 +168,8 @@
     )(queries, keys, grads, segments, segments.reshape(tokens, 1))
 
 
-def project_kernel(chips, steps, own_ref, other_ref, *rest):
-    row_refs, out_refs, gathered = rest[:chips], rest[-chips - 1:-1], rest[-1]
+def project_kernel(chips, steps, cuts, own_ref, other_ref, *rest):
+    row_refs, out_refs, gathered = rest[:chips], rest[-chips * (len(cuts) - 1) - 1:-1], rest[-1]
     taken, depth = row_refs[0].shape
     step = pl.program_id(0)
 
@@ -183,8 +183,9 @@
             gathered[...].reshape(chips * taken, depth), weight_ref[...], (((1,), (1,)), ((), ())),
             preferred_element_type=jnp.float32,
         ).astype(jnp.bfloat16)
-        for by in range(chips):
-            out_refs[by][...] = product[by * taken:(by + 1) * taken]
+        for part, (start, end) in enumerate(zip(cuts, cuts[1:])):
+            for by in range(chips):
+                out_refs[part * chips + by][...] = product[by * taken + start:by * taken + end]
 
     @pl.when(step < steps)
     def _():
@@ -195,24 +196,26 @@
         multiply(other_ref)
 
 
-def project(rows, own, other, after):
+def project(rows, own, other, cuts, after):
     chips = len(rows)
     taken, depth = rows[0].shape
     width = own.shape[0]
     block = min(width, 512)
     steps = width // block
-    return call(
-        functools.partial(project_kernel, chips, steps), "project",
+    counts = [end - start for start, end in zip(cuts, cuts[1:]) for by in range(chips)]
+    results = list(call(
+        functools.partial(project_kernel, chips, steps, cuts), "project",
         4 * chips * taken * depth * width, 2 * (chips * taken * (depth + 2 * width) + 2 * width * depth),
         grid=(CORES * steps,),
         in_specs=[
             pl.BlockSpec((block, depth), lambda i: (jnp.minimum(i, steps - 1), 0)),
             pl.BlockSpec((block, depth), lambda i: (jnp.maximum(i - steps, 0), 0)),
         ] + [pl.BlockSpec((taken, depth), lambda i: (0, 0))] * chips + [whole] * len(after),
-        out_specs=[pl.BlockSpec((taken, block), lambda i: (0, i))] * chips,
-        out_shape=[jax.ShapeDtypeStruct((taken, CORES * width), jnp.bfloat16)] * chips,
+        out_specs=[pl.BlockSpec((count, block), lambda i: (0, i)) for count in counts],
+        out_shape=[jax.ShapeDtypeStruct((count, CORES * width), jnp.bfloat16) for count in counts],
         scratch_shapes=[pltpu.VMEM((chips, taken, depth), jnp.bfloat16)],
-    )(own, other, *rows, *after)
+    )(own, other, *rows, *after))
+    return [results[at:at + chips] for at in range(0, len(results), chips)]
 
 
 def backward_kernel(chips, place_ref, x_ref, gain_ref, grad_ref, *rest):
@@ -242,26 +245,27 @@
         ).astype(out_ref.dtype)
 
 
-def norm_backward(place, cots, rows, gain, grads, after):
+def norm_backward(place, cots, rows, gain, grads, start, after):
     tokens, width = rows.shape
     taken, part_width = cots[0].shape
-    block = min(taken, 32)
+    block = math.gcd(math.gcd(start, taken), 32)
+    first = start // block
     return call(
         functools.partial(backward_kernel, len(cots)), "norm_backward",
         10 * taken * width, 8 * taken * width,
         grid=(taken // block,),
         in_specs=[
             scalars,
-            pl.BlockSpec((block, width), lambda i: (i, 0)),
+            pl.BlockSpec((block, width), lambda i: (first + i, 0)),
             pl.BlockSpec((1, width), lambda i: (0, 0)),
-            pl.BlockSpec((block, width), lambda i: (i, 0)),
+            pl.BlockSpec((block, width), lambda i: (first + i, 0)),
         ] + [pl.BlockSpec((block, part_width), lambda i: (i, 0))] * len(cots) + [whole] * len(after),
         out_specs=pl.BlockSpec((block, width), lambda i: (i, 0)),
         out_shape=jax.ShapeDtypeStruct((taken, width), jnp.bfloat16),
     )(place, rows, gain, grads, *cots, *after)
 
 
-def outer_kernel(groups, sums, *refs):
+def outer_kernel(groups, sums, halves, *refs):
     arrays = sum(groups)
     cots, columns, terms = refs[:arrays], refs[arrays:2 * arrays], refs[2 * arrays:2 * arrays + sums]
     total, at = None, 0
@@ -276,27 +280,38 @@
         total = product if total is None else total + product
     for term in terms:
         total += term[...].astype(jnp.float32)
+    if halves:
+        lower, upper = refs[2 * arrays + sums:2 * arrays + sums + 2]
+        in_lower = pl.program_id(0) < pl.num_programs(0) // 2
+        total += jnp.where(in_lower, lower[...], upper[...]).astype(jnp.float32)
     refs[-1][...] = total.astype(refs[-1].dtype)
 
 
-def outer(groups, cot_width, half, before, dtype):
+def outer(groups, cot_width, half, before, dtype, part=0, parts=1, halves=(), after=()):
     payloads = [payload for group in groups for payload in group]
     wide = payloads[0].shape[1]
     width = (wide - cot_width) // CORES
-    block = math.gcd(math.gcd(width, 256), cot_width)
-    first = (cot_width + half * width) // block
-    out_spec = pl.BlockSpec((block, cot_width), lambda i: (i, 0))
+    block = math.gcd(math.gcd(width // 2, 256), cot_width)
+    steps = width // parts // block
+    skip = part * steps
+    first = (cot_width + half * width) // block + skip
+    middle = steps // 2
     tokens = sum(payload.shape[0] for payload in payloads)
     return call(
-        functools.partial(outer_kernel, [len(group) for group in groups], len(before)), "outer",
+        functools.partial(outer_kernel, [len(group) for group in groups], len(before), len(halves)), "outer",
         2 * tokens * width * cot_width, 2 * tokens * width + 4 * width * cot_width,
-        grid=(width // block,),
+        grid=(steps,),
         in_specs=[pl.BlockSpec((payload.shape[0], cot_width), lambda i: (0, 0)) for payload in payloads]
         + [pl.BlockSpec((payload.shape[0], block), lambda i: (0, first + i)) for payload in payloads]
-        + [out_spec] * len(before),
-        out_specs=out_spec,
-        out_shape=jax.ShapeDtypeStruct((width, cot_width), dtype),
-    )(*payloads, *payloads, *before)
+        + [pl.BlockSpec((block, cot_width), lambda i: (skip + i, 0)) for term in before]
+        + [
+            pl.BlockSpec((block, cot_width), lambda i: (jnp.minimum(i, middle - 1), 0)),
+            pl.BlockSpec((block, cot_width), lambda i: (jnp.maximum(i - middle, 0), 0)),
+        ][:len(halves)]
+        + [whole] * len(after),
+        out_specs=pl.BlockSpec((block, cot_width), lambda i: (i, 0)),
+        out_shape=jax.ShapeDtypeStruct((width // parts, cot_width), dtype),
+    )(*payloads, *payloads, *before, *halves, *after)
 
 
 def shards(
@@ -336,24 +351,27 @@
         between_lines(moved[section * spread:(section + 1) * spread], 0, section) for section in range(1, sections)
     ]
 
-    parts = project(rows, kv_weight[0], other_weight, [joint])
-    arrived = [parts[0]] + [along_chips(parts[by], by, 1) for by in range(1, chips)]
-    kept = apply([middle], spread, tokens - spread, [parts[0]])
+    cuts = [0, tokens * 5 // 8, tokens]
+    parts = project(rows, kv_weight[0], other_weight, cuts, [joint])
+    arrived = [
+        [part[0]] + [along_chips(part[by], by, 1) for by in range(1, chips)] for part in parts
+    ]
+    backward = functools.partial(norm_backward, place, rows=frozen_input[0], gain=frozen_gain, grads=output_grad[0])
+    above = backward(arrived[0], start=cuts[0], after=columns[1:])
+    kept = apply([middle], spread, tokens - spread, [above] + arrived[1][1:])
     late = apply(near[1:], 0, tokens, kept)
-
-    input_cot = norm_backward(
-        place, arrived, frozen_input[0], frozen_gain, output_grad[0], late[:1] + returned[1:] + columns[1:]
-    )
-    cot_below = from_behind(input_cot, "pipe", -1)
+    above = [above, backward(arrived[1], start=cuts[1], after=late[:1] + returned[1:])]
+    below = [from_behind(half, "pipe", -1) for half in above]
+    cot_below = stack_rows(below, [])
 
     columns += [along_chips(block, by) for block, by in zip(late, near[1:])]
     last = along_chips(kept[0], middle)
 
     groups = [[column] for column in columns] + [returned]
-    sums = [outer(groups, kv_width, half, [], jnp.float32) for half in range(CORES)]
-    given = outer([[last]], kv_width, 1, [sums[1]], jnp.bfloat16)
-    taken = swap_cores(given)
-    grad = outer([[last]], kv_width, 0, [sums[0], taken], jnp.float32)
+    sums = [outer(groups, kv_width, half, [], jnp.float32, after=above[1:]) for half in range(CORES)]
+    given = [outer([[last]], kv_width, 1, [sums[1]], jnp.bfloat16, part, 2) for part in range(2)]
+    taken = [swap_cores(part) for part in given]
+    grad = outer([[last]], kv_width, 0, [sums[0]], jnp.float32, halves=taken, after=[cot_below])
     return (cot_below[None], grad[None])
 
 

time: 146 us -> 143 us (0.979); the launches traced: 146 us -> 141 us
  waiting for transfers between devices: 94 us -> 76.1 us
  starting transfers between devices: 19.1 us -> 29.1 us
  Pallas kernels: 25.6 us -> 28.4 us
    ppermute x9 -> x12, waiting for transfers between devices: 87.9 us -> 70 us  [along_chips(): return lax.ppermute(array, ('pipe', 'dp'), pairs)]
    ppermute x1 -> x2, starting transfers between devices: 1.92 us -> 7 us  [from_behind(): return lax.ppermute(array, axis, pairs)]
    ppermute x6, waiting for transfers between devices: 0.02 us -> 4.44 us  [between_lines(): return lax.ppermute(array, ('pipe', 'dp'), pairs)]
    ppermute x9 -> x12, starting transfers between devices: 10.9 us -> 15.1 us  [along_chips(): return lax.ppermute(array, ('pipe', 'dp'), pairs)]
    ppermute x1 -> x2, waiting for transfers between devices: 5.65 us -> 1.66 us  [from_behind(): return lax.ppermute(array, axis, pairs)]
    pallas_call x1 -> x2, Pallas kernels: 3.26 us -> 4.27 us  [norm_backward(): call(functools.partial(backward_kernel, len(cots)), 'norm_backward', 10 *...]
    unnamed x23 -> x24, local copies, waits for them, and re-layouts: 5.36 us -> 5.63 us
    pallas_call x4 -> x5, Pallas kernels: 7.75 us -> 7.76 us  [outer(): call(functools.partial(outer_kernel, [len(group) for group in groups], le...]
  transfers between devices with their start and end apart: 19 -> 24, of which waited for: 11 -> 12; matrix products, arithmetic and copies ran while one was open for 1% -> 1% of each run, Pallas kernels for 15% -> 18%
where the time goes in v2:
time: 143 us; the launch traced here: 141 us
  waiting for transfers between devices  76.1 us (53%)
  starting transfers between devices  29.1 us (20%)
  Pallas kernels  28.4 us (20%)
  local copies, waits for them, and re-layouts  6.44 us (5%)
    ppermute x12, waiting for transfers between devices, along_chips(): return lax.ppermute(array, ('pipe', 'dp'), pairs)  70 us
    ppermute x12, starting transfers between devices, along_chips(): return lax.ppermute(array, ('pipe', 'dp'), pairs)  15.1 us
    pallas_call x5, Pallas kernels, outer(): call(functools.partial(outer_kernel, [len(group) for group in groups], le...  7.76 us
    ppermute x2, starting transfers between devices, from_behind(): return lax.ppermute(array, axis, pairs)  7 us
    unnamed x24, local copies, waits for them, and re-layouts  5.63 us
    ppermute x6, starting transfers between devices, between_lines(): return lax.ppermute(array, ('pipe', 'dp'), pairs)  5.38 us
    pallas_call x1, Pallas kernels, project(): call(functools.partial(project_kernel, chips, steps, cuts), 'project', 4...  5.38 us
    pallas_call x4, Pallas kernels, normalize(): call(functools.partial(norm_kernel, chips, ahead), 'norm_forward', 4 * co...  5.04 us
  transfers between devices with their start and end apart: 24, of which 12 were waited for; matrix products, arithmetic and copies ran while one was open for 1% of the time, Pallas kernels for 18%

profile of v2, /device:TPU:10, one launch (start us, length us, event | category | flops | bytes accessed | tf_op | source)
XLA Modules:
  0.0 141.1 jit_solution(14578800923672192573)
XLA Ops:
  1.2 2.6 %collective-permute-start.2 = (bf16[128,1024]{1,0:T(8,128)(2,1)}, bf16[128,1024]{1,0:T(8,128)(2,1)S(1)}, u32[]{:S(2)}, u32[]{:S(2)}) collective-permute-start(bf16[128,1024]{1,0:T(8,128)(2,1)} %bitcast.29), channel_id=1, source_target_pairs={{0,1},{1,0},{2,3},{3,2},{4,5},{5,4},{6,7},{7,6},{8,12},{9,13},{10,... | collective-permute-start | bytes 786440 | tf_op jit(solution)/shard_map/ppermute | solution.py:34
  3.8 2.5 %collective-permute-start.3 = (bf16[128,1024]{1,0:T(8,128)(2,1)}, bf16[128,1024]{1,0:T(8,128)(2,1)S(1)}, u32[]{:S(2)}, u32[]{:S(2)}) collective-permute-start(bf16[128,1024]{1,0:T(8,128)(2,1)} %bitcast.30), channel_id=1, source_target_pairs={{0,1},{1,0},{2,3},{3,2},{4,5},{5,4},{6,7},{7,6},{8,10},{9,11},{10,... | collective-permute-start | bytes 786440 | tf_op jit(solution)/shard_map/ppermute | solution.py:34
  6.3 0.8 copy.13.col_seg_ref
  7.1 1.2 copy-done.4
  8.3 1.2 copy-done.5
  9.5 0.9 copy-done.8
  10.4 0.7 copy-done.9
  11.1 4.5 %attend.1.cot_ref = bf16[128,512]{1,0:T(8,128)(2,1)S(1)} custom-call(bf16[128,4096]{1,0:T(8,128)(2,1)S(1)} %bitcast.22, bf16[128,512]{1,0:T(8,128)(2,1)S(1)} %bitcast.24, bf16[128,4096]{1,0:T(8,128)(2,1)S(1)} %bitcast.23, s32[1,128]{1,0:T(1,128)S(1)} %copy-done.9, s32[128,1]{1,0:T(8,128)S(1)} %copy.13.col_seg_ref), custom_call_target="tpu_custom_call" | custom-call | flops 268435456 | bytes 2097152 | tf_op jit(solution)/shard_map/attend/pallas_call | solution.py:155
  15.6 0.8 norm_forward.4.refs_0_
  16.4 1.4 %collective-permute-start.4 = (bf16[32,2560]{1,0:T(8,128)(2,1)S(1)}, bf16[32,2560]{1,0:T(8,128)(2,1)S(1)}, u32[]{:S(2)}, u32[]{:S(2)}) collective-permute-start(bf16[32,2560]{1,0:T(8,128)(2,1)S(1)} %norm_forward.4.refs_0_), channel_id=1, source_target_pairs={{8,0},{9,1},{10,2},{11,3},{12,4},{13,5},{14,6},{15,7}} | collective-permute-start | bytes 491528 | tf_op jit(solution)/shard_map/ppermute | solution.py:40
  17.9 0.7 collective-permute-start.5
  18.6 0.7 collective-permute-start.6
  19.2 2.8 %collective-permute-done.2.rest_1_.rest_2_ = bf16[128,1024]{1,0:T(8,128)(2,1)S(1)} collective-permute-done((bf16[128,1024]{1,0:T(8,128)(2,1)}, bf16[128,1024]{1,0:T(8,128)(2,1)S(1)}, u32[]{:S(2)}, u32[]{:S(2)}) %collective-permute-start.2) | collective-permute-done | bytes 262176 | tf_op jit(solution)/shard_map/ppermute | solution.py:34
  22.1 4.8 %collective-permute-done.3.rest_2_.rest_3_ = bf16[128,1024]{1,0:T(8,128)(2,1)S(1)} collective-permute-done((bf16[128,1024]{1,0:T(8,128)(2,1)}, bf16[128,1024]{1,0:T(8,128)(2,1)S(1)}, u32[]{:S(2)}, u32[]{:S(2)}) %collective-permute-start.3) | collective-permute-done | bytes 262176 | tf_op jit(solution)/shard_map/ppermute | solution.py:34
  26.9 1.5 %norm_forward.5 = (bf16[128,2560]{1,0:T(8,128)(2,1)S(1)}, bf16[128,2560]{1,0:T(8,128)(2,1)S(1)}) custom-call(s32[2]{0:T(128)S(1)} %pad_add_fusion.place_ref, bf16[128,8192]{1,0:T(8,128)(2,1)S(1)} %bitcast.14, bf16[1,8192]{1,0:T(2,128)(2,1)S(1)} %copy-done.6, bf16[128,512]{1,0:T(8,128)(2,1)S(1)} %attend.1.cot_ref, ...), custom_call_target="tpu_custom_call" | custom-call | flops 4194304 | bytes 3407872 | tf_op jit(solution)/shard_map/norm_forward/pallas_call | solution.py:92
  28.5 2.4 %collective-permute-start.10 = (bf16[128,2560]{1,0:T(8,128)(2,1)S(1)}, bf16[128,2560]{1,0:T(8,128)(2,1)S(1)}, u32[]{:S(2)}, u32[]{:S(2)}) collective-permute-start(bf16[128,2560]{1,0:T(8,128)(2,1)S(1)} %get-tuple-element.17), channel_id=1, source_target_pairs={{0,2},{1,3},{2,4},{3,5},{4,6},{5,7},{6,0},{7,1},{8,10},{9,11},{10,... | collective-permute-start | bytes 1966088 | tf_op jit(solution)/shard_map/ppermute | solution.py:34
  31.0 0.8 collective-permute-start.15
  31.9 5.4 %project.1 = (bf16[80,2048]{1,0:T(8,128)(2,1)S(1)}, bf16[80,2048]{1,0:T(8,128)(2,1)S(1)}, bf16[80,2048]{1,0:T(8,128)(2,1)S(1)}, bf16[80,2048]{1,0:T(8,128)(2,1)S...) custom-call(bf16[1024,1024]{1,0:T(8,128)(2,1)S(1)} %bitcast.27, ...), custom_call_target="tpu_custom_call" | custom-call | flops 2147483648 | bytes 7340032 | tf_op jit(solution)/shard_map/project/pallas_call | solution.py:206
  37.3 2.0 %collective-permute-start.8 = (bf16[80,2048]{1,0:T(8,128)(2,1)S(1)}, bf16[80,2048]{1,0:T(8,128)(2,1)S(1)}, u32[]{:S(2)}, u32[]{:S(2)}) collective-permute-start(bf16[80,2048]{1,0:T(8,128)(2,1)S(1)} %get-tuple-element.15), channel_id=1, source_target_pairs={{0,1},{1,0},{2,3},{3,2},{4,5},{5,4},{6,7},{7,6},{8,12},{9,13},{10,... | collective-permute-start | bytes 983048 | tf_op jit(solution)/shard_map/ppermute | solution.py:34
  39.3 1.0 collective-permute-start.9
  40.3 5.8 %collective-permute-done.10.rest_4_.refs_1_.refs_8_ = bf16[128,2560]{1,0:T(8,128)(2,1)S(1)} collective-permute-done((bf16[128,2560]{1,0:T(8,128)(2,1)S(1)}, bf16[128,2560]{1,0:T(8,128)(2,1)S(1)}, u32[]{:S(2)}, u32[]{:S(2)}) %collective-permute-start.10) | collective-permute-done | bytes 655392 | tf_op jit(solution)/shard_map/ppermute | solution.py:34
  46.2 2.4 %collective-permute-start.12 = (bf16[48,2048]{1,0:T(8,128)(2,1)S(1)}, bf16[48,2048]{1,0:T(8,128)(2,1)S(1)}, u32[]{:S(2)}, u32[]{:S(2)}) collective-permute-start(bf16[48,2048]{1,0:T(8,128)(2,1)S(1)} %get-tuple-element.19), channel_id=1, source_target_pairs={{0,1},{1,0},{2,3},{3,2},{4,5},{5,4},{6,7},{7,6},{8,10},{9,11},{10,... | collective-permute-start | bytes 589832 | tf_op jit(solution)/shard_map/ppermute | solution.py:34
  48.6 18.6 %collective-permute-done.7.rest_1_ = bf16[80,2048]{1,0:T(8,128)(2,1)S(1)} collective-permute-done((bf16[80,2048]{1,0:T(8,128)(2,1)S(1)}, bf16[80,2048]{1,0:T(8,128)(2,1)S(1)}, u32[]{:S(2)}, u32[]{:S(2)}) %collective-permute-start.7) | collective-permute-done | bytes 327712 | tf_op jit(solution)/shard_map/ppermute | solution.py:34
  67.2 11.2 %collective-permute-done.8.rest_2_ = bf16[80,2048]{1,0:T(8,128)(2,1)S(1)} collective-permute-done((bf16[80,2048]{1,0:T(8,128)(2,1)S(1)}, bf16[80,2048]{1,0:T(8,128)(2,1)S(1)}, u32[]{:S(2)}, u32[]{:S(2)}) %collective-permute-start.8) | collective-permute-done | bytes 327712 | tf_op jit(solution)/shard_map/ppermute | solution.py:34
  78.4 4.4 %collective-permute-done.9.rest_3_ = bf16[80,2048]{1,0:T(8,128)(2,1)S(1)} collective-permute-done((bf16[80,2048]{1,0:T(8,128)(2,1)S(1)}, bf16[80,2048]{1,0:T(8,128)(2,1)S(1)}, u32[]{:S(2)}, u32[]{:S(2)}) %collective-permute-start.9) | collective-permute-done | bytes 327712 | tf_op jit(solution)/shard_map/ppermute | solution.py:34
  82.8 2.5 %norm_backward.2.rest_0_ = bf16[80,8192]{1,0:T(8,128)(2,1)S(1)} custom-call(s32[2]{0:T(128)S(1)} %pad_add_fusion.place_ref, bf16[128,8192]{1,0:T(8,128)(2,1)S(1)} %bitcast.17, bf16[1,8192]{1,0:T(2,128)(2,1)S(1)} %copy-done.7, bf16[128,8192]{1,0:T(8,128)(2,1)S(1)} %bitcast.19, bf16[80,2048]{1,0:T(8,128)(2,1)S(1)} %get-tuple-element.13.rest_0_, ...), custom_call_target="tpu_custom_call" | custom-call | flops 6553600 | bytes 5242880 | tf_op jit(solution)/shard_map/norm_backward/pallas_call | solution.py:253
  85.4 1.9 %collective-permute-start.11 = (bf16[80,8192]{1,0:T(8,128)(2,1)S(1)}, bf16[80,8192]{1,0:T(8,128)(2,1)S(1)}, u32[]{:S(2)}, u32[]{:S(2)}) collective-permute-start(bf16[80,8192]{1,0:T(8,128)(2,1)S(1)} %norm_backward.2.rest_0_), channel_id=1, source_target_pairs={{8,0},{16,8},{24,16},{9,1},{17,9},{25,17},{10,2},{18,10},{26,18},{... | collective-permute-start | bytes 3932168 | tf_op jit(solution)/shard_map/ppermute | solution.py:25
  87.3 2.0 %collective-permute-done.13.rest_2_ = bf16[48,2048]{1,0:T(8,128)(2,1)S(1)} collective-permute-done((bf16[48,2048]{1,0:T(8,128)(2,1)S(1)}, bf16[48,2048]{1,0:T(8,128)(2,1)S(1)}, u32[]{:S(2)}, u32[]{:S(2)}) %collective-permute-start.13) | collective-permute-done | bytes 196640 | tf_op jit(solution)/shard_map/ppermute | solution.py:34
  89.3 1.8 %collective-permute-done.14.rest_3_ = bf16[48,2048]{1,0:T(8,128)(2,1)S(1)} collective-permute-done((bf16[48,2048]{1,0:T(8,128)(2,1)S(1)}, bf16[48,2048]{1,0:T(8,128)(2,1)S(1)}, u32[]{:S(2)}, u32[]{:S(2)}) %collective-permute-start.14) | collective-permute-done | bytes 196640 | tf_op jit(solution)/shard_map/ppermute | solution.py:34
  91.2 1.2 norm_forward.6.rest_0_
  92.4 1.5 %norm_forward.7.rest_4_ = bf16[128,2560]{1,0:T(8,128)(2,1)S(1)} custom-call(s32[2]{0:T(128)S(1)} %pad_add_fusion.place_ref, bf16[128,8192]{1,0:T(8,128)(2,1)S(1)} %bitcast.16, bf16[1,8192]{1,0:T(2,128)(2,1)S(1)} %copy-done.6, bf16[128,512]{1,0:T(8,128)(2,1)S(1)} %attend.1.cot_ref, bf16[96,2560]{1,0:T(8,128)(2,1)S(1)} %norm_forward.6.rest_0_), custom_call_target="tpu_custom_call" | custom-call | flops 4194304 | bytes 2752512 | tf_op jit(solution)/shard_map/norm_forward/pallas_call | solution.py:92
  94.1 1.3 collective-permute-start.16
  95.4 1.6 %collective-permute-start.20 = (bf16[96,2560]{1,0:T(8,128)(2,1)S(1)}, bf16[96,2560]{1,0:T(8,128)(2,1)S(1)}, u32[]{:S(2)}, u32[]{:S(2)}) collective-permute-start(bf16[96,2560]{1,0:T(8,128)(2,1)S(1)} %norm_forward.6.rest_0_), channel_id=1, source_target_pairs={{0,4},{1,5},{2,6},{3,7},{4,0},{5,1},{6,2},{7,3},{8,12},{9,13},{10,... | collective-permute-start | bytes 1474568 | tf_op jit(solution)/shard_map/ppermute | solution.py:34
  97.0 0.7 collective-permute-start.17
  97.6 4.4 %collective-permute-done.16.rest_5_.refs_4_.refs_11_ = bf16[32,2560]{1,0:T(8,128)(2,1)S(1)} collective-permute-done((bf16[32,2560]{1,0:T(8,128)(2,1)S(1)}, bf16[32,2560]{1,0:T(8,128)(2,1)S(1)}, u32[]{:S(2)}, u32[]{:S(2)}) %collective-permute-start.16) | collective-permute-done | bytes 163872 | tf_op jit(solution)/shard_map/ppermute | solution.py:40
  102.1 0.7 collective-permute-start.18
  102.8 1.7 %norm_backward.3.refs_14_ = bf16[48,8192]{1,0:T(8,128)(2,1)S(1)} custom-call(s32[2]{0:T(128)S(1)} %pad_add_fusion.place_ref, bf16[128,8192]{1,0:T(8,128)(2,1)S(1)} %bitcast.18, bf16[1,8192]{1,0:T(2,128)(2,1)S(1)} %copy-done.7, bf16[128,8192]{1,0:T(8,128)(2,1)S(1)} %bitcast.20, bf16[48,2048]{1,0:T(8,128)(2,1)S(1)} %get-tuple-element.18.rest_0_, ...), custom_call_target="tpu_custom_call" | custom-call | flops 3932160 | bytes 3145728 | tf_op jit(solution)/shard_map/norm_backward/pallas_call | solution.py:253
  104.5 5.1 %collective-permute-start.19 = (bf16[48,8192]{1,0:T(8,128)(2,1)S(1)}, bf16[48,8192]{1,0:T(8,128)(2,1)S(1)}, u32[]{:S(2)}, u32[]{:S(2)}) collective-permute-start(bf16[48,8192]{1,0:T(8,128)(2,1)S(1)} %norm_backward.3.refs_14_), channel_id=1, source_target_pairs={{8,0},{16,8},{24,16},{9,1},{17,9},{25,17},{10,2},{18,10},{26,18},{... | collective-permute-start | bytes 2359304 | tf_op jit(solution)/shard_map/ppermute | solution.py:25
  109.6 12.5 %collective-permute-done.21.refs_2_.refs_9_ = bf16[128,2560]{1,0:T(8,128)(2,1)S(1)} collective-permute-done((bf16[128,2560]{1,0:T(8,128)(2,1)S(1)}, bf16[128,2560]{1,0:T(8,128)(2,1)S(1)}, u32[]{:S(2)}, u32[]{:S(2)}) %collective-permute-start.21) | collective-permute-done | bytes 655392 | tf_op jit(solution)/shard_map/ppermute | solution.py:34
  122.1 2.1 %outer.6.refs_2_ = f32[1024,512]{1,0:T(8,128)S(1)} custom-call(bf16[128,2560]{1,0:T(8,128)(2,1)S(1)} %get-tuple-element.12.refs_4_.refs_0_.refs_7_, bf16[128,2560]{1,0:T(8,128)(2,1)S(1)} %collective-permute-done.10.rest_4_.refs_1_.refs_8_, bf16[128,2560]{1,0:T(8,128)(2,1)S(1)} %collective-permute-done.21.refs_2_.refs_9_, ...), custom_call_target="tpu_custom_call" | custom-call | flops 536870912 | bytes 3145728 | tf_op jit(solution)/shard_map/outer/pallas_call | solution.py:300
  124.2 5.8 %collective-permute-done.20.refs_0_.refs_1_ = bf16[96,2560]{1,0:T(8,128)(2,1)S(1)} collective-permute-done((bf16[96,2560]{1,0:T(8,128)(2,1)S(1)}, bf16[96,2560]{1,0:T(8,128)(2,1)S(1)}, u32[]{:S(2)}, u32[]{:S(2)}) %collective-permute-start.20) | collective-permute-done | bytes 491552 | tf_op jit(solution)/shard_map/ppermute | solution.py:34
  130.1 0.5 outer.8
  130.7 0.6 outer.7
  131.8 2.1 %outer.5.refs_2_ = f32[1024,512]{1,0:T(8,128)S(1)} custom-call(bf16[128,2560]{1,0:T(8,128)(2,1)S(1)} %get-tuple-element.12.refs_4_.refs_0_.refs_7_, bf16[128,2560]{1,0:T(8,128)(2,1)S(1)} %collective-permute-done.10.rest_4_.refs_1_.refs_8_, bf16[128,2560]{1,0:T(8,128)(2,1)S(1)} %collective-permute-done.21.refs_2_.refs_9_, ...), custom_call_target="tpu_custom_call" | custom-call | flops 536870912 | bytes 3145728 | tf_op jit(solution)/shard_map/outer/pallas_call | solution.py:300
  134.0 1.7 %collective-permute-done.19.refs_1_ = bf16[48,8192]{1,0:T(8,128)(2,1)S(1)} collective-permute-done((bf16[48,8192]{1,0:T(8,128)(2,1)S(1)}, bf16[48,8192]{1,0:T(8,128)(2,1)S(1)}, u32[]{:S(2)}, u32[]{:S(2)}) %collective-permute-start.19) | collective-permute-done | bytes 786464 | tf_op jit(solution)/shard_map/ppermute | solution.py:25
  135.6 1.5 %stack_rows.3.refs_5_ = bf16[128,8192]{1,0:T(8,128)(2,1)} custom-call(bf16[80,8192]{1,0:T(8,128)(2,1)S(1)} %collective-permute-done.11.refs_0_, bf16[48,8192]{1,0:T(8,128)(2,1)S(1)} %collective-permute-done.19.refs_1_), custom_call_target="tpu_custom_call" | custom-call | bytes 4194304 | tf_op jit(solution)/shard_map/stack_rows/pallas_call | solution.py:117
  137.1 1.6 %copy-done.3 = bf16[128,8192]{1,0:T(8,128)(2,1)S(1)} copy-done((bf16[128,8192]{1,0:T(8,128)(2,1)S(1)}, bf16[128,8192]{1,0:T(8,128)(2,1)}, u32[]{:S(2)}) %copy-start.3) | copy-done | bytes 2097176
  138.7 2.4 %outer.9 = f32[1024,512]{1,0:T(8,128)} custom-call(bf16[96,2560]{1,0:T(8,128)(2,1)S(1)} %collective-permute-done.20.refs_0_.refs_1_, bf16[96,2560]{1,0:T(8,128)(2,1)S(1)} %collective-permute-done.20.refs_0_.refs_1_, f32[1024,512]{1,0:T(8,128)S(1)} %outer.5.refs_2_, bf16[512,512]{1,0:T(8,128)(2,1)S(1)} %collective-permute-done.22.refs_3_, ...), custom_call_target="tpu_custom_call" | custom-call | flops 100663296 | bytes 2293760 | tf_op jit(solution)/shard_map/outer/pallas_call | solution.py:300
  (42 shorter events, 1.6 us)
Async XLA Ops:
  0.6 15.0 %copy-start = (bf16[1,128,8192]{2,1,0:T(8,128)(2,1)S(1)}, bf16[1,128,8192]{2,1,0:T(8,128)(2,1)}, u32[]{:S(2)}) copy-start(bf16[1,128,8192]{2,1,0:T(8,128)(2,1)} %param.11) | copy-start | bytes 6291460
  0.6 15.0 %collective-permute-start = (bf16[1024,1024]{1,0:T(8,128)(2,1)}, bf16[1024,1024]{1,0:T(8,128)(2,1)}, u32[]{:S(2)}, u32[]{:S(2)}) collective-permute-start(bf16[1024,1024]{1,0:T(8,128)(2,1)} %bitcast.26), channel_id=1, source_target_pairs={{0,1},{1,0},{2,3},{3,2},{4,5},{5,4},{6,7},{7,6},{8,9},{9,8},{10,11... | collective-permute-start | bytes 6291464 | tf_op jit(solution)/shard_map/ppermute | solution.py:51
  0.7 17.8 %collective-permute-start.1 = (bf16[128,1024]{1,0:T(8,128)(2,1)}, bf16[128,1024]{1,0:T(8,128)(2,1)S(1)}, u32[]{:S(2)}, u32[]{:S(2)}) collective-permute-start(bf16[128,1024]{1,0:T(8,128)(2,1)} %bitcast.28), channel_id=1, source_target_pairs={{0,1},{1,0},{2,3},{3,2},{4,5},{5,4},{6,7},{7,6},{8,14},{9,15},{10,... | collective-permute-start | bytes 786440 | tf_op jit(solution)/shard_map/ppermute | solution.py:34
  1.2 20.8 %collective-permute-start.2 = (bf16[128,1024]{1,0:T(8,128)(2,1)}, bf16[128,1024]{1,0:T(8,128)(2,1)S(1)}, u32[]{:S(2)}, u32[]{:S(2)}) collective-permute-start(bf16[128,1024]{1,0:T(8,128)(2,1)} %bitcast.29), channel_id=1, source_target_pairs={{0,1},{1,0},{2,3},{3,2},{4,5},{5,4},{6,7},{7,6},{8,12},{9,13},{10,... | collective-permute-start | bytes 786440 | tf_op jit(solution)/shard_map/ppermute | solution.py:34
  3.8 23.1 %collective-permute-start.3 = (bf16[128,1024]{1,0:T(8,128)(2,1)}, bf16[128,1024]{1,0:T(8,128)(2,1)S(1)}, u32[]{:S(2)}, u32[]{:S(2)}) collective-permute-start(bf16[128,1024]{1,0:T(8,128)(2,1)} %bitcast.30), channel_id=1, source_target_pairs={{0,1},{1,0},{2,3},{3,2},{4,5},{5,4},{6,7},{7,6},{8,10},{9,11},{10,... | collective-permute-start | bytes 786440 | tf_op jit(solution)/shard_map/ppermute | solution.py:34
  7.1 1.2 copy-start.4
  8.3 1.2 copy-start.5
  9.5 0.9 copy-start.8
  10.4 0.7 copy-start.9
  11.1 4.6 %copy-start.6 = (bf16[1,8192]{1,0:T(2,128)(2,1)S(1)}, bf16[1,8192]{1,0:T(2,128)(2,1)}, u32[]{:S(2)}) copy-start(bf16[1,8192]{1,0:T(2,128)(2,1)} %gain_ref.10) | copy-start | bytes 49156
  16.4 15.4 %copy-start.10 = (bf16[1,1024,1024]{2,1,0:T(8,128)(2,1)S(1)}, bf16[1,1024,1024]{2,1,0:T(8,128)(2,1)}, u32[]{:S(2)}) copy-start(bf16[1,1024,1024]{2,1,0:T(8,128)(2,1)} %param.21) | copy-start | bytes 6291460
  16.4 15.4 %copy-start.11 = (bf16[1,128,1024]{2,1,0:T(8,128)(2,1)S(1)}, bf16[1,128,1024]{2,1,0:T(8,128)(2,1)}, u32[]{:S(2)}) copy-start(bf16[1,128,1024]{2,1,0:T(8,128)(2,1)} %param.20) | copy-start | bytes 786436
  16.4 14.5 %collective-permute-start.4 = (bf16[32,2560]{1,0:T(8,128)(2,1)S(1)}, bf16[32,2560]{1,0:T(8,128)(2,1)S(1)}, u32[]{:S(2)}, u32[]{:S(2)}) collective-permute-start(bf16[32,2560]{1,0:T(8,128)(2,1)S(1)} %norm_forward.4.refs_0_), channel_id=1, source_target_pairs={{8,0},{9,1},{10,2},{11,3},{12,4},{13,5},{14,6},{15,7}} | collective-permute-start | bytes 491528 | tf_op jit(solution)/shard_map/ppermute | solution.py:40
  17.9 13.0 %collective-permute-start.5 = (bf16[32,2560]{1,0:T(8,128)(2,1)S(1)}, bf16[32,2560]{1,0:T(8,128)(2,1)S(1)}, u32[]{:S(2)}, u32[]{:S(2)}) collective-permute-start(bf16[32,2560]{1,0:T(8,128)(2,1)S(1)} %norm_forward.4.refs_0_), channel_id=1, source_target_pairs={{16,0},{17,1},{18,2},{19,3},{20,4},{21,5},{22,6},{23,7}} | collective-permute-start | bytes 491528 | tf_op jit(solution)/shard_map/ppermute | solution.py:40
  18.6 12.3 %collective-permute-start.6 = (bf16[32,2560]{1,0:T(8,128)(2,1)S(1)}, bf16[32,2560]{1,0:T(8,128)(2,1)S(1)}, u32[]{:S(2)}, u32[]{:S(2)}) collective-permute-start(bf16[32,2560]{1,0:T(8,128)(2,1)S(1)} %norm_forward.4.refs_0_), channel_id=1, source_target_pairs={{24,0},{25,1},{26,2},{27,3},{28,4},{29,5},{30,6},{31,7}} | collective-permute-start | bytes 491528 | tf_op jit(solution)/shard_map/ppermute | solution.py:40
  28.5 17.7 %collective-permute-start.10 = (bf16[128,2560]{1,0:T(8,128)(2,1)S(1)}, bf16[128,2560]{1,0:T(8,128)(2,1)S(1)}, u32[]{:S(2)}, u32[]{:S(2)}) collective-permute-start(bf16[128,2560]{1,0:T(8,128)(2,1)S(1)} %get-tuple-element.17), channel_id=1, source_target_pairs={{0,2},{1,3},{2,4},{3,5},{4,6},{5,7},{6,0},{7,1},{8,10},{9,11},{10,... | collective-permute-start | bytes 1966088 | tf_op jit(solution)/shard_map/ppermute | solution.py:34
  31.0 51.9 %copy-start.1 = (bf16[1,128,8192]{2,1,0:T(8,128)(2,1)S(1)}, bf16[1,128,8192]{2,1,0:T(8,128)(2,1)}, u32[]{:S(2)}) copy-start(bf16[1,128,8192]{2,1,0:T(8,128)(2,1)} %param.17) | copy-start | bytes 6291460
  31.0 51.9 %copy-start.2 = (bf16[1,128,8192]{2,1,0:T(8,128)(2,1)S(1)}, bf16[1,128,8192]{2,1,0:T(8,128)(2,1)}, u32[]{:S(2)}) copy-start(bf16[1,128,8192]{2,1,0:T(8,128)(2,1)} %param.19) | copy-start | bytes 6291460
  31.0 51.9 %copy-start.7 = (bf16[1,8192]{1,0:T(2,128)(2,1)S(1)}, bf16[1,8192]{1,0:T(2,128)(2,1)}, u32[]{:S(2)}) copy-start(bf16[1,8192]{1,0:T(2,128)(2,1)} %gain_ref.11) | copy-start | bytes 49156
  31.0 63.0 %collective-permute-start.15 = (bf16[128,2560]{1,0:T(8,128)(2,1)S(1)}, bf16[128,2560]{1,0:T(8,128)(2,1)S(1)}, u32[]{:S(2)}, u32[]{:S(2)}) collective-permute-start(bf16[128,2560]{1,0:T(8,128)(2,1)S(1)} %stack_rows.2.rest_4_), channel_id=1, source_target_pairs={{0,4},{1,5},{2,6},{3,7},{4,0},{5,1},{6,2},{7,3}} | collective-permute-start | bytes 1966088 | tf_op jit(solution)/shard_map/ppermute | solution.py:46
  37.2 29.9 %collective-permute-start.7 = (bf16[80,2048]{1,0:T(8,128)(2,1)S(1)}, bf16[80,2048]{1,0:T(8,128)(2,1)S(1)}, u32[]{:S(2)}, u32[]{:S(2)}) collective-permute-start(bf16[80,2048]{1,0:T(8,128)(2,1)S(1)} %get-tuple-element.14), channel_id=1, source_target_pairs={{0,1},{1,0},{2,3},{3,2},{4,5},{5,4},{6,7},{7,6},{8,10},{9,11},{10,... | collective-permute-start | bytes 983048 | tf_op jit(solution)/shard_map/ppermute | solution.py:34
  37.3 41.1 %collective-permute-start.8 = (bf16[80,2048]{1,0:T(8,128)(2,1)S(1)}, bf16[80,2048]{1,0:T(8,128)(2,1)S(1)}, u32[]{:S(2)}, u32[]{:S(2)}) collective-permute-start(bf16[80,2048]{1,0:T(8,128)(2,1)S(1)} %get-tuple-element.15), channel_id=1, source_target_pairs={{0,1},{1,0},{2,3},{3,2},{4,5},{5,4},{6,7},{7,6},{8,12},{9,13},{10,... | collective-permute-start | bytes 983048 | tf_op jit(solution)/shard_map/ppermute | solution.py:34
  39.3 43.5 %collective-permute-start.9 = (bf16[80,2048]{1,0:T(8,128)(2,1)S(1)}, bf16[80,2048]{1,0:T(8,128)(2,1)S(1)}, u32[]{:S(2)}, u32[]{:S(2)}) collective-permute-start(bf16[80,2048]{1,0:T(8,128)(2,1)S(1)} %get-tuple-element.16), channel_id=1, source_target_pairs={{0,1},{1,0},{2,3},{3,2},{4,5},{5,4},{6,7},{7,6},{8,14},{9,15},{10,... | collective-permute-start | bytes 983048 | tf_op jit(solution)/shard_map/ppermute | solution.py:34
  46.2 41.1 %collective-permute-start.12 = (bf16[48,2048]{1,0:T(8,128)(2,1)S(1)}, bf16[48,2048]{1,0:T(8,128)(2,1)S(1)}, u32[]{:S(2)}, u32[]{:S(2)}) collective-permute-start(bf16[48,2048]{1,0:T(8,128)(2,1)S(1)} %get-tuple-element.19), channel_id=1, source_target_pairs={{0,1},{1,0},{2,3},{3,2},{4,5},{5,4},{6,7},{7,6},{8,10},{9,11},{10,... | collective-permute-start | bytes 589832 | tf_op jit(solution)/shard_map/ppermute | solution.py:34
  67.2 22.2 %collective-permute-start.13 = (bf16[48,2048]{1,0:T(8,128)(2,1)S(1)}, bf16[48,2048]{1,0:T(8,128)(2,1)S(1)}, u32[]{:S(2)}, u32[]{:S(2)}) collective-permute-start(bf16[48,2048]{1,0:T(8,128)(2,1)S(1)} %get-tuple-element.20), channel_id=1, source_target_pairs={{0,1},{1,0},{2,3},{3,2},{4,5},{5,4},{6,7},{7,6},{8,12},{9,13},{10,... | collective-permute-start | bytes 589832 | tf_op jit(solution)/shard_map/ppermute | solution.py:34
  78.4 12.8 %collective-permute-start.14 = (bf16[48,2048]{1,0:T(8,128)(2,1)S(1)}, bf16[48,2048]{1,0:T(8,128)(2,1)S(1)}, u32[]{:S(2)}, u32[]{:S(2)}) collective-permute-start(bf16[48,2048]{1,0:T(8,128)(2,1)S(1)} %get-tuple-element.21), channel_id=1, source_target_pairs={{0,1},{1,0},{2,3},{3,2},{4,5},{5,4},{6,7},{7,6},{8,14},{9,15},{10,... | collective-permute-start | bytes 589832 | tf_op jit(solution)/shard_map/ppermute | solution.py:34
  85.4 50.3 %collective-permute-start.11 = (bf16[80,8192]{1,0:T(8,128)(2,1)S(1)}, bf16[80,8192]{1,0:T(8,128)(2,1)S(1)}, u32[]{:S(2)}, u32[]{:S(2)}) collective-permute-start(bf16[80,8192]{1,0:T(8,128)(2,1)S(1)} %norm_backward.2.rest_0_), channel_id=1, source_target_pairs={{8,0},{16,8},{24,16},{9,1},{17,9},{25,17},{10,2},{18,10},{26,18},{... | collective-permute-start | bytes 3932168 | tf_op jit(solution)/shard_map/ppermute | solution.py:25
  93.9 28.2 %collective-permute-start.21 = (bf16[128,2560]{1,0:T(8,128)(2,1)S(1)}, bf16[128,2560]{1,0:T(8,128)(2,1)S(1)}, u32[]{:S(2)}, u32[]{:S(2)}) collective-permute-start(bf16[128,2560]{1,0:T(8,128)(2,1)S(1)} %norm_forward.7.rest_4_), channel_id=1, source_target_pairs={{0,6},{1,7},{2,0},{3,1},{4,2},{5,3},{6,4},{7,5},{8,14},{9,15},{10,... | collective-permute-start | bytes 1966088 | tf_op jit(solution)/shard_map/ppermute | solution.py:34
  94.1 8.0 %collective-permute-start.16 = (bf16[32,2560]{1,0:T(8,128)(2,1)S(1)}, bf16[32,2560]{1,0:T(8,128)(2,1)S(1)}, u32[]{:S(2)}, u32[]{:S(2)}) collective-permute-start(bf16[32,2560]{1,0:T(8,128)(2,1)S(1)} %get-tuple-element.25), channel_id=1, source_target_pairs={{0,8},{1,9},{2,10},{3,11},{4,12},{5,13},{6,14},{7,15}} | collective-permute-start | bytes 491528 | tf_op jit(solution)/shard_map/ppermute | solution.py:40
  95.4 34.7 %collective-permute-start.20 = (bf16[96,2560]{1,0:T(8,128)(2,1)S(1)}, bf16[96,2560]{1,0:T(8,128)(2,1)S(1)}, u32[]{:S(2)}, u32[]{:S(2)}) collective-permute-start(bf16[96,2560]{1,0:T(8,128)(2,1)S(1)} %norm_forward.6.rest_0_), channel_id=1, source_target_pairs={{0,4},{1,5},{2,6},{3,7},{4,0},{5,1},{6,2},{7,3},{8,12},{9,13},{10,... | collective-permute-start | bytes 1474568 | tf_op jit(solution)/shard_map/ppermute | solution.py:34
  97.0 5.8 %collective-permute-start.17 = (bf16[32,2560]{1,0:T(8,128)(2,1)S(1)}, bf16[32,2560]{1,0:T(8,128)(2,1)S(1)}, u32[]{:S(2)}, u32[]{:S(2)}) collective-permute-start(bf16[32,2560]{1,0:T(8,128)(2,1)S(1)} %get-tuple-element.24), channel_id=1, source_target_pairs={{0,16},{1,17},{2,18},{3,19},{4,20},{5,21},{6,22},{7,23}} | collective-permute-start | bytes 491528 | tf_op jit(solution)/shard_map/ppermute | solution.py:40
  102.1 0.7 collective-permute-start.18
  104.5 31.1 %collective-permute-start.19 = (bf16[48,8192]{1,0:T(8,128)(2,1)S(1)}, bf16[48,8192]{1,0:T(8,128)(2,1)S(1)}, u32[]{:S(2)}, u32[]{:S(2)}) collective-permute-start(bf16[48,8192]{1,0:T(8,128)(2,1)S(1)} %norm_backward.3.refs_14_), channel_id=1, source_target_pairs={{8,0},{16,8},{24,16},{9,1},{17,9},{25,17},{10,2},{18,10},{26,18},{... | collective-permute-start | bytes 2359304 | tf_op jit(solution)/shard_map/ppermute | solution.py:25
  130.6 6.5 %collective-permute-start.23 = (bf16[512,512]{1,0:T(8,128)(2,1)S(1)}, bf16[512,512]{1,0:T(8,128)(2,1)S(1)}, u32[]{:S(2)}, u32[]{:S(2)}) collective-permute-start(bf16[512,512]{1,0:T(8,128)(2,1)S(1)} %outer.8), channel_id=1, source_target_pairs={{0,1},{1,0},{2,3},{3,2},{4,5},{5,4},{6,7},{7,6},{8,9},{9,8},{10,11... | collective-permute-start | bytes 1572872 | tf_op jit(solution)/shard_map/ppermute | solution.py:51
  131.3 5.8 %collective-permute-start.22 = (bf16[512,512]{1,0:T(8,128)(2,1)S(1)}, bf16[512,512]{1,0:T(8,128)(2,1)S(1)}, u32[]{:S(2)}, u32[]{:S(2)}) collective-permute-start(bf16[512,512]{1,0:T(8,128)(2,1)S(1)} %outer.7), channel_id=1, source_target_pairs={{0,1},{1,0},{2,3},{3,2},{4,5},{5,4},{6,7},{7,6},{8,9},{9,8},{10,11... | collective-permute-start | bytes 1572872 | tf_op jit(solution)/shard_map/ppermute | solution.py:51
  137.1 1.6 %copy-start.3 = (bf16[128,8192]{1,0:T(8,128)(2,1)S(1)}, bf16[128,8192]{1,0:T(8,128)(2,1)}, u32[]{:S(2)}) copy-start(bf16[128,8192]{1,0:T(8,128)(2,1)} %stack_rows.3.refs_5_) | copy-start | bytes 6291460

commit v3 on v2

--- a/solution.py
+++ b/solution.py
@@ -358,9 +358,9 @@
     ]
     backward = functools.partial(norm_backward, place, rows=frozen_input[0], gain=frozen_gain, grads=output_grad[0])
     above = backward(arrived[0], start=cuts[0], after=columns[1:])
-    kept = apply([middle], spread, tokens - spread, [above] + arrived[1][1:])
+    kept = apply([middle], spread, tokens - spread, [above] + [arrived[1][by] for by in near])
     late = apply(near[1:], 0, tokens, kept)
-    above = [above, backward(arrived[1], start=cuts[1], after=late[:1] + returned[1:])]
+    above = [above, backward(arrived[1], start=cuts[1], after=late[:1])]
     below = [from_behind(half, "pipe", -1) for half in above]
     cot_below = stack_rows(below, [])
 
@@ -369,7 +369,7 @@
 
     groups = [[column] for column in columns] + [returned]
     sums = [outer(groups, kv_width, half, [], jnp.float32, after=above[1:]) for half in range(CORES)]
-    given = [outer([[last]], kv_width, 1, [sums[1]], jnp.bfloat16, part, 2) for part in range(2)]
+    given = [outer([[last]], kv_width, 1, sums[1:], jnp.bfloat16, part, 2, after=sums[:1]) for part in range(2)]
     taken = [swap_cores(part) for part in given]
     grad = outer([[last]], kv_width, 0, [sums[0]], jnp.float32, halves=taken, after=[cot_below])
     return (cot_below[None], grad[None])

time: 143 us -> 143 us (level)
  waiting for transfers between devices: 76.1 us -> 72.6 us
  starting transfers between devices: 29.1 us -> 32.2 us
    ppermute x6, waiting for transfers between devices: 4.44 us -> 0.02 us  [between_lines(): return lax.ppermute(array, ('pipe', 'dp'), pairs)]
    ppermute x12, starting transfers between devices: 15.1 us -> 17.2 us  [along_chips(): return lax.ppermute(array, ('pipe', 'dp'), pairs)]
  transfers between devices with their start and end apart: 24 -> 24, of which waited for: 12 -> 8; matrix products, arithmetic and copies ran while one was open for 1% -> 1% of each run, Pallas kernels for 18% -> 19%
where the time goes in v3:
time: 143 us; the launch traced here: 141 us
  waiting for transfers between devices  72.6 us (51%)
  starting transfers between devices  32.2 us (23%)
  Pallas kernels  28.5 us (20%)
  local copies, waits for them, and re-layouts  6.44 us (5%)
    ppermute x12, waiting for transfers between devices, along_chips(): return lax.ppermute(array, ('pipe', 'dp'), pairs)  69.7 us
    ppermute x12, starting transfers between devices, along_chips(): return lax.ppermute(array, ('pipe', 'dp'), pairs)  17.2 us
    ppermute x2, starting transfers between devices, from_behind(): return lax.ppermute(array, axis, pairs)  8.05 us
    pallas_call x5, Pallas kernels, outer(): call(functools.partial(outer_kernel, [len(group) for group in groups], le...  7.85 us
    unnamed x24, local copies, waits for them, and re-layouts  5.63 us
    ppermute x6, starting transfers between devices, between_lines(): return lax.ppermute(array, ('pipe', 'dp'), pairs)  5.4 us
    pallas_call x1, Pallas kernels, project(): call(functools.partial(project_kernel, chips, steps, cuts), 'project', 4...  5.38 us
    pallas_call x4, Pallas kernels, normalize(): call(functools.partial(norm_kernel, chips, ahead), 'norm_forward', 4 * co...  5.06 us
  transfers between devices with their start and end apart: 24, of which 8 were waited for; matrix products, arithmetic and copies ran while one was open for 1% of the time, Pallas kernels for 19%

profile of v3, /device:TPU:10, one launch (start us, length us, event | category | flops | bytes accessed | tf_op | source)
XLA Modules:
  0.0 140.8 jit_solution(11002508604778175948)
XLA Ops:
  0.7 0.5 collective-permute-start.1
  1.2 2.6 %collective-permute-start.2 = (bf16[128,1024]{1,0:T(8,128)(2,1)}, bf16[128,1024]{1,0:T(8,128)(2,1)S(1)}, u32[]{:S(2)}, u32[]{:S(2)}) collective-permute-start(bf16[128,1024]{1,0:T(8,128)(2,1)} %bitcast.29), channel_id=1, source_target_pairs={{0,1},{1,0},{2,3},{3,2},{4,5},{5,4},{6,7},{7,6},{8,12},{9,13},{10,... | collective-permute-start | bytes 786440 | tf_op jit(solution)/shard_map/ppermute | solution.py:34
  3.8 2.5 %collective-permute-start.3 = (bf16[128,1024]{1,0:T(8,128)(2,1)}, bf16[128,1024]{1,0:T(8,128)(2,1)S(1)}, u32[]{:S(2)}, u32[]{:S(2)}) collective-permute-start(bf16[128,1024]{1,0:T(8,128)(2,1)} %bitcast.30), channel_id=1, source_target_pairs={{0,1},{1,0},{2,3},{3,2},{4,5},{5,4},{6,7},{7,6},{8,10},{9,11},{10,... | collective-permute-start | bytes 786440 | tf_op jit(solution)/shard_map/ppermute | solution.py:34
  6.3 0.8 copy.13.col_seg_ref
  7.1 1.2 copy-done.4
  8.3 1.2 copy-done.5
  9.5 0.9 copy-done.8
  10.4 0.7 copy-done.9
  11.1 4.5 %attend.1.cot_ref = bf16[128,512]{1,0:T(8,128)(2,1)S(1)} custom-call(bf16[128,4096]{1,0:T(8,128)(2,1)S(1)} %bitcast.22, bf16[128,512]{1,0:T(8,128)(2,1)S(1)} %bitcast.24, bf16[128,4096]{1,0:T(8,128)(2,1)S(1)} %bitcast.23, s32[1,128]{1,0:T(1,128)S(1)} %copy-done.9, s32[128,1]{1,0:T(8,128)S(1)} %copy.13.col_seg_ref), custom_call_target="tpu_custom_call" | custom-call | flops 268435456 | bytes 2097152 | tf_op jit(solution)/shard_map/attend/pallas_call | solution.py:155
  15.6 0.8 norm_forward.4.refs_0_
  16.4 1.4 %collective-permute-start.4 = (bf16[32,2560]{1,0:T(8,128)(2,1)S(1)}, bf16[32,2560]{1,0:T(8,128)(2,1)S(1)}, u32[]{:S(2)}, u32[]{:S(2)}) collective-permute-start(bf16[32,2560]{1,0:T(8,128)(2,1)S(1)} %norm_forward.4.refs_0_), channel_id=1, source_target_pairs={{8,0},{9,1},{10,2},{11,3},{12,4},{13,5},{14,6},{15,7}} | collective-permute-start | bytes 491528 | tf_op jit(solution)/shard_map/ppermute | solution.py:40
  17.9 0.7 collective-permute-start.5
  18.6 0.7 collective-permute-start.6
  19.2 2.8 %collective-permute-done.2.rest_1_.rest_2_ = bf16[128,1024]{1,0:T(8,128)(2,1)S(1)} collective-permute-done((bf16[128,1024]{1,0:T(8,128)(2,1)}, bf16[128,1024]{1,0:T(8,128)(2,1)S(1)}, u32[]{:S(2)}, u32[]{:S(2)}) %collective-permute-start.2) | collective-permute-done | bytes 262176 | tf_op jit(solution)/shard_map/ppermute | solution.py:34
  22.1 4.8 %collective-permute-done.3.rest_2_.rest_3_ = bf16[128,1024]{1,0:T(8,128)(2,1)S(1)} collective-permute-done((bf16[128,1024]{1,0:T(8,128)(2,1)}, bf16[128,1024]{1,0:T(8,128)(2,1)S(1)}, u32[]{:S(2)}, u32[]{:S(2)}) %collective-permute-start.3) | collective-permute-done | bytes 262176 | tf_op jit(solution)/shard_map/ppermute | solution.py:34
  26.9 1.5 %norm_forward.5 = (bf16[128,2560]{1,0:T(8,128)(2,1)S(1)}, bf16[128,2560]{1,0:T(8,128)(2,1)S(1)}) custom-call(s32[2]{0:T(128)S(1)} %pad_add_fusion.place_ref, bf16[128,8192]{1,0:T(8,128)(2,1)S(1)} %bitcast.14, bf16[1,8192]{1,0:T(2,128)(2,1)S(1)} %copy-done.6, bf16[128,512]{1,0:T(8,128)(2,1)S(1)} %attend.1.cot_ref, ...), custom_call_target="tpu_custom_call" | custom-call | flops 4194304 | bytes 3407872 | tf_op jit(solution)/shard_map/norm_forward/pallas_call | solution.py:92
  28.5 2.4 %collective-permute-start.10 = (bf16[128,2560]{1,0:T(8,128)(2,1)S(1)}, bf16[128,2560]{1,0:T(8,128)(2,1)S(1)}, u32[]{:S(2)}, u32[]{:S(2)}) collective-permute-start(bf16[128,2560]{1,0:T(8,128)(2,1)S(1)} %get-tuple-element.17), channel_id=1, source_target_pairs={{0,2},{1,3},{2,4},{3,5},{4,6},{5,7},{6,0},{7,1},{8,10},{9,11},{10,... | collective-permute-start | bytes 1966088 | tf_op jit(solution)/shard_map/ppermute | solution.py:34
  31.0 0.8 collective-permute-start.18
  31.9 5.4 %project.1 = (bf16[80,2048]{1,0:T(8,128)(2,1)S(1)}, bf16[80,2048]{1,0:T(8,128)(2,1)S(1)}, bf16[80,2048]{1,0:T(8,128)(2,1)S(1)}, bf16[80,2048]{1,0:T(8,128)(2,1)S...) custom-call(bf16[1024,1024]{1,0:T(8,128)(2,1)S(1)} %bitcast.27, ...), custom_call_target="tpu_custom_call" | custom-call | flops 2147483648 | bytes 7340032 | tf_op jit(solution)/shard_map/project/pallas_call | solution.py:206
  37.2 0.1 collective-permute-start.7
  37.3 2.0 %collective-permute-start.8 = (bf16[80,2048]{1,0:T(8,128)(2,1)S(1)}, bf16[80,2048]{1,0:T(8,128)(2,1)S(1)}, u32[]{:S(2)}, u32[]{:S(2)}) collective-permute-start(bf16[80,2048]{1,0:T(8,128)(2,1)S(1)} %get-tuple-element.15), channel_id=1, source_target_pairs={{0,1},{1,0},{2,3},{3,2},{4,5},{5,4},{6,7},{7,6},{8,12},{9,13},{10,... | collective-permute-start | bytes 983048 | tf_op jit(solution)/shard_map/ppermute | solution.py:34
  39.3 1.0 collective-permute-start.9
  40.3 5.8 %collective-permute-done.10.rest_4_.refs_1_.refs_8_ = bf16[128,2560]{1,0:T(8,128)(2,1)S(1)} collective-permute-done((bf16[128,2560]{1,0:T(8,128)(2,1)S(1)}, bf16[128,2560]{1,0:T(8,128)(2,1)S(1)}, u32[]{:S(2)}, u32[]{:S(2)}) %collective-permute-start.10) | collective-permute-done | bytes 655392 | tf_op jit(solution)/shard_map/ppermute | solution.py:34
  46.2 2.4 %collective-permute-start.12 = (bf16[48,2048]{1,0:T(8,128)(2,1)S(1)}, bf16[48,2048]{1,0:T(8,128)(2,1)S(1)}, u32[]{:S(2)}, u32[]{:S(2)}) collective-permute-start(bf16[48,2048]{1,0:T(8,128)(2,1)S(1)} %get-tuple-element.19), channel_id=1, source_target_pairs={{0,1},{1,0},{2,3},{3,2},{4,5},{5,4},{6,7},{7,6},{8,10},{9,11},{10,... | collective-permute-start | bytes 589832 | tf_op jit(solution)/shard_map/ppermute | solution.py:34
  48.6 18.6 %collective-permute-done.7.rest_1_ = bf16[80,2048]{1,0:T(8,128)(2,1)S(1)} collective-permute-done((bf16[80,2048]{1,0:T(8,128)(2,1)S(1)}, bf16[80,2048]{1,0:T(8,128)(2,1)S(1)}, u32[]{:S(2)}, u32[]{:S(2)}) %collective-permute-start.7) | collective-permute-done | bytes 327712 | tf_op jit(solution)/shard_map/ppermute | solution.py:34
  67.2 15.4 %collective-permute-done.8.rest_2_ = bf16[80,2048]{1,0:T(8,128)(2,1)S(1)} collective-permute-done((bf16[80,2048]{1,0:T(8,128)(2,1)S(1)}, bf16[80,2048]{1,0:T(8,128)(2,1)S(1)}, u32[]{:S(2)}, u32[]{:S(2)}) %collective-permute-start.8) | collective-permute-done | bytes 327712 | tf_op jit(solution)/shard_map/ppermute | solution.py:34
  82.6 3.4 %collective-permute-start.13 = (bf16[48,2048]{1,0:T(8,128)(2,1)S(1)}, bf16[48,2048]{1,0:T(8,128)(2,1)S(1)}, u32[]{:S(2)}, u32[]{:S(2)}) collective-permute-start(bf16[48,2048]{1,0:T(8,128)(2,1)S(1)} %get-tuple-element.20), channel_id=1, source_target_pairs={{0,1},{1,0},{2,3},{3,2},{4,5},{5,4},{6,7},{7,6},{8,12},{9,13},{10,... | collective-permute-start | bytes 589832 | tf_op jit(solution)/shard_map/ppermute | solution.py:34
  86.0 2.5 %norm_backward.2.rest_0_ = bf16[80,8192]{1,0:T(8,128)(2,1)S(1)} custom-call(s32[2]{0:T(128)S(1)} %pad_add_fusion.place_ref, bf16[128,8192]{1,0:T(8,128)(2,1)S(1)} %bitcast.17, bf16[1,8192]{1,0:T(2,128)(2,1)S(1)} %copy-done.7, bf16[128,8192]{1,0:T(8,128)(2,1)S(1)} %bitcast.19, bf16[80,2048]{1,0:T(8,128)(2,1)S(1)} %get-tuple-element.13.rest_0_, ...), custom_call_target="tpu_custom_call" | custom-call | flops 6553600 | bytes 5242880 | tf_op jit(solution)/shard_map/norm_backward/pallas_call | solution.py:253
  88.5 1.9 %collective-permute-start.11 = (bf16[80,8192]{1,0:T(8,128)(2,1)S(1)}, bf16[80,8192]{1,0:T(8,128)(2,1)S(1)}, u32[]{:S(2)}, u32[]{:S(2)}) collective-permute-start(bf16[80,8192]{1,0:T(8,128)(2,1)S(1)} %norm_backward.2.rest_0_), channel_id=1, source_target_pairs={{8,0},{16,8},{24,16},{9,1},{17,9},{25,17},{10,2},{18,10},{26,18},{... | collective-permute-start | bytes 3932168 | tf_op jit(solution)/shard_map/ppermute | solution.py:25
  90.5 1.3 norm_forward.6.rest_0_
  91.8 1.5 %norm_forward.7.rest_4_ = bf16[128,2560]{1,0:T(8,128)(2,1)S(1)} custom-call(s32[2]{0:T(128)S(1)} %pad_add_fusion.place_ref, bf16[128,8192]{1,0:T(8,128)(2,1)S(1)} %bitcast.16, bf16[1,8192]{1,0:T(2,128)(2,1)S(1)} %copy-done.6, bf16[128,512]{1,0:T(8,128)(2,1)S(1)} %attend.1.cot_ref, bf16[96,2560]{1,0:T(8,128)(2,1)S(1)} %norm_forward.6.rest_0_), custom_call_target="tpu_custom_call" | custom-call | flops 4194304 | bytes 2752512 | tf_op jit(solution)/shard_map/norm_forward/pallas_call | solution.py:92
  93.3 0.3 collective-permute-start.17
  93.7 1.3 collective-permute-start.19
  95.0 19.8 %collective-permute-done.13.rest_2_ = bf16[48,2048]{1,0:T(8,128)(2,1)S(1)} collective-permute-done((bf16[48,2048]{1,0:T(8,128)(2,1)S(1)}, bf16[48,2048]{1,0:T(8,128)(2,1)S(1)}, u32[]{:S(2)}, u32[]{:S(2)}) %collective-permute-start.13) | collective-permute-done | bytes 196640 | tf_op jit(solution)/shard_map/ppermute | solution.py:34
  114.7 0.7 collective-permute-start.20
  115.4 0.7 collective-permute-start.21
  116.1 1.7 %norm_backward.3.refs_14_ = bf16[48,8192]{1,0:T(8,128)(2,1)S(1)} custom-call(s32[2]{0:T(128)S(1)} %pad_add_fusion.place_ref, bf16[128,8192]{1,0:T(8,128)(2,1)S(1)} %bitcast.18, bf16[1,8192]{1,0:T(2,128)(2,1)S(1)} %copy-done.7, bf16[128,8192]{1,0:T(8,128)(2,1)S(1)} %bitcast.20, bf16[48,2048]{1,0:T(8,128)(2,1)S(1)} %get-tuple-element.18.rest_0_, ...), custom_call_target="tpu_custom_call" | custom-call | flops 3932160 | bytes 3145728 | tf_op jit(solution)/shard_map/norm_backward/pallas_call | solution.py:253
  117.8 6.1 %collective-permute-start.15 = (bf16[48,8192]{1,0:T(8,128)(2,1)S(1)}, bf16[48,8192]{1,0:T(8,128)(2,1)S(1)}, u32[]{:S(2)}, u32[]{:S(2)}) collective-permute-start(bf16[48,8192]{1,0:T(8,128)(2,1)S(1)} %norm_backward.3.refs_14_), channel_id=1, source_target_pairs={{8,0},{16,8},{24,16},{9,1},{17,9},{25,17},{10,2},{18,10},{26,18},{... | collective-permute-start | bytes 2359304 | tf_op jit(solution)/shard_map/ppermute | solution.py:25
  124.0 2.4 %collective-permute-done.17.refs_2_.refs_9_ = bf16[128,2560]{1,0:T(8,128)(2,1)S(1)} collective-permute-done((bf16[128,2560]{1,0:T(8,128)(2,1)S(1)}, bf16[128,2560]{1,0:T(8,128)(2,1)S(1)}, u32[]{:S(2)}, u32[]{:S(2)}) %collective-permute-start.17) | collective-permute-done | bytes 655392 | tf_op jit(solution)/shard_map/ppermute | solution.py:34
  126.4 2.1 %outer.6.refs_2_ = f32[1024,512]{1,0:T(8,128)S(1)} custom-call(bf16[128,2560]{1,0:T(8,128)(2,1)S(1)} %get-tuple-element.12.refs_4_.refs_0_.refs_7_, bf16[128,2560]{1,0:T(8,128)(2,1)S(1)} %collective-permute-done.10.rest_4_.refs_1_.refs_8_, bf16[128,2560]{1,0:T(8,128)(2,1)S(1)} %collective-permute-done.17.refs_2_.refs_9_, ...), custom_call_target="tpu_custom_call" | custom-call | flops 536870912 | bytes 3145728 | tf_op jit(solution)/shard_map/outer/pallas_call | solution.py:300
  128.5 2.1 %outer.5.refs_3_.refs_2_ = f32[1024,512]{1,0:T(8,128)S(1)} custom-call(bf16[128,2560]{1,0:T(8,128)(2,1)S(1)} %get-tuple-element.12.refs_4_.refs_0_.refs_7_, bf16[128,2560]{1,0:T(8,128)(2,1)S(1)} %collective-permute-done.10.rest_4_.refs_1_.refs_8_, bf16[128,2560]{1,0:T(8,128)(2,1)S(1)} %collective-permute-done.17.refs_2_.refs_9_, ...), custom_call_target="tpu_custom_call" | custom-call | flops 536870912 | bytes 3145728 | tf_op jit(solution)/shard_map/outer/pallas_call | solution.py:300
  130.7 0.6 outer.8
  131.3 0.6 outer.7
  131.9 0.5 collective-permute-start.22
  132.5 2.8 %collective-permute-done.15.refs_1_ = bf16[48,8192]{1,0:T(8,128)(2,1)S(1)} collective-permute-done((bf16[48,8192]{1,0:T(8,128)(2,1)S(1)}, bf16[48,8192]{1,0:T(8,128)(2,1)S(1)}, u32[]{:S(2)}, u32[]{:S(2)}) %collective-permute-start.15) | collective-permute-done | bytes 786464 | tf_op jit(solution)/shard_map/ppermute | solution.py:25
  135.3 1.5 %stack_rows.3.refs_5_ = bf16[128,8192]{1,0:T(8,128)(2,1)} custom-call(bf16[80,8192]{1,0:T(8,128)(2,1)S(1)} %collective-permute-done.11.refs_0_, bf16[48,8192]{1,0:T(8,128)(2,1)S(1)} %collective-permute-done.15.refs_1_), custom_call_target="tpu_custom_call" | custom-call | bytes 4194304 | tf_op jit(solution)/shard_map/stack_rows/pallas_call | solution.py:117
  136.8 1.6 %copy-done.3 = bf16[128,8192]{1,0:T(8,128)(2,1)S(1)} copy-done((bf16[128,8192]{1,0:T(8,128)(2,1)S(1)}, bf16[128,8192]{1,0:T(8,128)(2,1)}, u32[]{:S(2)}) %copy-start.3) | copy-done | bytes 2097176
  138.4 2.4 %outer.9 = f32[1024,512]{1,0:T(8,128)} custom-call(bf16[96,2560]{1,0:T(8,128)(2,1)S(1)} %collective-permute-done.16.refs_0_.refs_1_, bf16[96,2560]{1,0:T(8,128)(2,1)S(1)} %collective-permute-done.16.refs_0_.refs_1_, f32[1024,512]{1,0:T(8,128)S(1)} %outer.5.refs_3_.refs_2_, bf16[512,512]{1,0:T(8,128)(2,1)S(1)} %collective-permute-done.22.refs_3_, ...), custom_call_target="tpu_custom_call" | custom-call | flops 100663296 | bytes 2293760 | tf_op jit(solution)/shard_map/outer/pallas_call | solution.py:300
  (42 shorter events, 0.5 us)
Async XLA Ops:
  0.6 15.0 %copy-start = (bf16[1,128,8192]{2,1,0:T(8,128)(2,1)S(1)}, bf16[1,128,8192]{2,1,0:T(8,128)(2,1)}, u32[]{:S(2)}) copy-start(bf16[1,128,8192]{2,1,0:T(8,128)(2,1)} %param.11) | copy-start | bytes 6291460
  0.6 15.0 %collective-permute-start = (bf16[1024,1024]{1,0:T(8,128)(2,1)}, bf16[1024,1024]{1,0:T(8,128)(2,1)}, u32[]{:S(2)}, u32[]{:S(2)}) collective-permute-start(bf16[1024,1024]{1,0:T(8,128)(2,1)} %bitcast.26), channel_id=1, source_target_pairs={{0,1},{1,0},{2,3},{3,2},{4,5},{5,4},{6,7},{7,6},{8,9},{9,8},{10,11... | collective-permute-start | bytes 6291464 | tf_op jit(solution)/shard_map/ppermute | solution.py:51
  0.7 17.8 %collective-permute-start.1 = (bf16[128,1024]{1,0:T(8,128)(2,1)}, bf16[128,1024]{1,0:T(8,128)(2,1)S(1)}, u32[]{:S(2)}, u32[]{:S(2)}) collective-permute-start(bf16[128,1024]{1,0:T(8,128)(2,1)} %bitcast.28), channel_id=1, source_target_pairs={{0,1},{1,0},{2,3},{3,2},{4,5},{5,4},{6,7},{7,6},{8,14},{9,15},{10,... | collective-permute-start | bytes 786440 | tf_op jit(solution)/shard_map/ppermute | solution.py:34
  1.2 20.8 %collective-permute-start.2 = (bf16[128,1024]{1,0:T(8,128)(2,1)}, bf16[128,1024]{1,0:T(8,128)(2,1)S(1)}, u32[]{:S(2)}, u32[]{:S(2)}) collective-permute-start(bf16[128,1024]{1,0:T(8,128)(2,1)} %bitcast.29), channel_id=1, source_target_pairs={{0,1},{1,0},{2,3},{3,2},{4,5},{5,4},{6,7},{7,6},{8,12},{9,13},{10,... | collective-permute-start | bytes 786440 | tf_op jit(solution)/shard_map/ppermute | solution.py:34
  3.8 23.1 %collective-permute-start.3 = (bf16[128,1024]{1,0:T(8,128)(2,1)}, bf16[128,1024]{1,0:T(8,128)(2,1)S(1)}, u32[]{:S(2)}, u32[]{:S(2)}) collective-permute-start(bf16[128,1024]{1,0:T(8,128)(2,1)} %bitcast.30), channel_id=1, source_target_pairs={{0,1},{1,0},{2,3},{3,2},{4,5},{5,4},{6,7},{7,6},{8,10},{9,11},{10,... | collective-permute-start | bytes 786440 | tf_op jit(solution)/shard_map/ppermute | solution.py:34
  7.1 1.2 copy-start.4
  8.3 1.2 copy-start.5
  9.5 0.9 copy-start.8
  10.4 0.7 copy-start.9
  11.1 4.6 %copy-start.6 = (bf16[1,8192]{1,0:T(2,128)(2,1)S(1)}, bf16[1,8192]{1,0:T(2,128)(2,1)}, u32[]{:S(2)}) copy-start(bf16[1,8192]{1,0:T(2,128)(2,1)} %gain_ref.10) | copy-start | bytes 49156
  16.4 15.4 %copy-start.10 = (bf16[1,1024,1024]{2,1,0:T(8,128)(2,1)S(1)}, bf16[1,1024,1024]{2,1,0:T(8,128)(2,1)}, u32[]{:S(2)}) copy-start(bf16[1,1024,1024]{2,1,0:T(8,128)(2,1)} %param.21) | copy-start | bytes 6291460
  16.4 15.4 %copy-start.11 = (bf16[1,128,1024]{2,1,0:T(8,128)(2,1)S(1)}, bf16[1,128,1024]{2,1,0:T(8,128)(2,1)}, u32[]{:S(2)}) copy-start(bf16[1,128,1024]{2,1,0:T(8,128)(2,1)} %param.20) | copy-start | bytes 786436
  16.4 14.5 %collective-permute-start.4 = (bf16[32,2560]{1,0:T(8,128)(2,1)S(1)}, bf16[32,2560]{1,0:T(8,128)(2,1)S(1)}, u32[]{:S(2)}, u32[]{:S(2)}) collective-permute-start(bf16[32,2560]{1,0:T(8,128)(2,1)S(1)} %norm_forward.4.refs_0_), channel_id=1, source_target_pairs={{8,0},{9,1},{10,2},{11,3},{12,4},{13,5},{14,6},{15,7}} | collective-permute-start | bytes 491528 | tf_op jit(solution)/shard_map/ppermute | solution.py:40
  17.9 13.0 %collective-permute-start.5 = (bf16[32,2560]{1,0:T(8,128)(2,1)S(1)}, bf16[32,2560]{1,0:T(8,128)(2,1)S(1)}, u32[]{:S(2)}, u32[]{:S(2)}) collective-permute-start(bf16[32,2560]{1,0:T(8,128)(2,1)S(1)} %norm_forward.4.refs_0_), channel_id=1, source_target_pairs={{16,0},{17,1},{18,2},{19,3},{20,4},{21,5},{22,6},{23,7}} | collective-permute-start | bytes 491528 | tf_op jit(solution)/shard_map/ppermute | solution.py:40
  18.6 12.3 %collective-permute-start.6 = (bf16[32,2560]{1,0:T(8,128)(2,1)S(1)}, bf16[32,2560]{1,0:T(8,128)(2,1)S(1)}, u32[]{:S(2)}, u32[]{:S(2)}) collective-permute-start(bf16[32,2560]{1,0:T(8,128)(2,1)S(1)} %norm_forward.4.refs_0_), channel_id=1, source_target_pairs={{24,0},{25,1},{26,2},{27,3},{28,4},{29,5},{30,6},{31,7}} | collective-permute-start | bytes 491528 | tf_op jit(solution)/shard_map/ppermute | solution.py:40
  28.5 17.7 %collective-permute-start.10 = (bf16[128,2560]{1,0:T(8,128)(2,1)S(1)}, bf16[128,2560]{1,0:T(8,128)(2,1)S(1)}, u32[]{:S(2)}, u32[]{:S(2)}) collective-permute-start(bf16[128,2560]{1,0:T(8,128)(2,1)S(1)} %get-tuple-element.17), channel_id=1, source_target_pairs={{0,2},{1,3},{2,4},{3,5},{4,6},{5,7},{6,0},{7,1},{8,10},{9,11},{10,... | collective-permute-start | bytes 1966088 | tf_op jit(solution)/shard_map/ppermute | solution.py:34
  31.0 55.0 %copy-start.1 = (bf16[1,128,8192]{2,1,0:T(8,128)(2,1)S(1)}, bf16[1,128,8192]{2,1,0:T(8,128)(2,1)}, u32[]{:S(2)}) copy-start(bf16[1,128,8192]{2,1,0:T(8,128)(2,1)} %param.17) | copy-start | bytes 6291460
  31.0 55.0 %copy-start.2 = (bf16[1,128,8192]{2,1,0:T(8,128)(2,1)S(1)}, bf16[1,128,8192]{2,1,0:T(8,128)(2,1)}, u32[]{:S(2)}) copy-start(bf16[1,128,8192]{2,1,0:T(8,128)(2,1)} %param.19) | copy-start | bytes 6291460
  31.0 55.0 %copy-start.7 = (bf16[1,8192]{1,0:T(2,128)(2,1)S(1)}, bf16[1,8192]{1,0:T(2,128)(2,1)}, u32[]{:S(2)}) copy-start(bf16[1,8192]{1,0:T(2,128)(2,1)} %gain_ref.11) | copy-start | bytes 49156
  31.0 62.6 %collective-permute-start.18 = (bf16[128,2560]{1,0:T(8,128)(2,1)S(1)}, bf16[128,2560]{1,0:T(8,128)(2,1)S(1)}, u32[]{:S(2)}, u32[]{:S(2)}) collective-permute-start(bf16[128,2560]{1,0:T(8,128)(2,1)S(1)} %stack_rows.2.rest_4_), channel_id=1, source_target_pairs={{0,4},{1,5},{2,6},{3,7},{4,0},{5,1},{6,2},{7,3}} | collective-permute-start | bytes 1966088 | tf_op jit(solution)/shard_map/ppermute | solution.py:46
  37.2 29.9 %collective-permute-start.7 = (bf16[80,2048]{1,0:T(8,128)(2,1)S(1)}, bf16[80,2048]{1,0:T(8,128)(2,1)S(1)}, u32[]{:S(2)}, u32[]{:S(2)}) collective-permute-start(bf16[80,2048]{1,0:T(8,128)(2,1)S(1)} %get-tuple-element.14), channel_id=1, source_target_pairs={{0,1},{1,0},{2,3},{3,2},{4,5},{5,4},{6,7},{7,6},{8,10},{9,11},{10,... | collective-permute-start | bytes 983048 | tf_op jit(solution)/shard_map/ppermute | solution.py:34
  37.3 45.3 %collective-permute-start.8 = (bf16[80,2048]{1,0:T(8,128)(2,1)S(1)}, bf16[80,2048]{1,0:T(8,128)(2,1)S(1)}, u32[]{:S(2)}, u32[]{:S(2)}) collective-permute-start(bf16[80,2048]{1,0:T(8,128)(2,1)S(1)} %get-tuple-element.15), channel_id=1, source_target_pairs={{0,1},{1,0},{2,3},{3,2},{4,5},{5,4},{6,7},{7,6},{8,12},{9,13},{10,... | collective-permute-start | bytes 983048 | tf_op jit(solution)/shard_map/ppermute | solution.py:34
  39.3 46.7 %collective-permute-start.9 = (bf16[80,2048]{1,0:T(8,128)(2,1)S(1)}, bf16[80,2048]{1,0:T(8,128)(2,1)S(1)}, u32[]{:S(2)}, u32[]{:S(2)}) collective-permute-start(bf16[80,2048]{1,0:T(8,128)(2,1)S(1)} %get-tuple-element.16), channel_id=1, source_target_pairs={{0,1},{1,0},{2,3},{3,2},{4,5},{5,4},{6,7},{7,6},{8,14},{9,15},{10,... | collective-permute-start | bytes 983048 | tf_op jit(solution)/shard_map/ppermute | solution.py:34
  46.2 44.3 %collective-permute-start.12 = (bf16[48,2048]{1,0:T(8,128)(2,1)S(1)}, bf16[48,2048]{1,0:T(8,128)(2,1)S(1)}, u32[]{:S(2)}, u32[]{:S(2)}) collective-permute-start(bf16[48,2048]{1,0:T(8,128)(2,1)S(1)} %get-tuple-element.19), channel_id=1, source_target_pairs={{0,1},{1,0},{2,3},{3,2},{4,5},{5,4},{6,7},{7,6},{8,10},{9,11},{10,... | collective-permute-start | bytes 589832 | tf_op jit(solution)/shard_map/ppermute | solution.py:34
  67.2 23.3 %collective-permute-start.14 = (bf16[48,2048]{1,0:T(8,128)(2,1)S(1)}, bf16[48,2048]{1,0:T(8,128)(2,1)S(1)}, u32[]{:S(2)}, u32[]{:S(2)}) collective-permute-start(bf16[48,2048]{1,0:T(8,128)(2,1)S(1)} %get-tuple-element.21), channel_id=1, source_target_pairs={{0,1},{1,0},{2,3},{3,2},{4,5},{5,4},{6,7},{7,6},{8,14},{9,15},{10,... | collective-permute-start | bytes 589832 | tf_op jit(solution)/shard_map/ppermute | solution.py:34
  82.6 32.1 %collective-permute-start.13 = (bf16[48,2048]{1,0:T(8,128)(2,1)S(1)}, bf16[48,2048]{1,0:T(8,128)(2,1)S(1)}, u32[]{:S(2)}, u32[]{:S(2)}) collective-permute-start(bf16[48,2048]{1,0:T(8,128)(2,1)S(1)} %get-tuple-element.20), channel_id=1, source_target_pairs={{0,1},{1,0},{2,3},{3,2},{4,5},{5,4},{6,7},{7,6},{8,12},{9,13},{10,... | collective-permute-start | bytes 589832 | tf_op jit(solution)/shard_map/ppermute | solution.py:34
  88.5 46.8 %collective-permute-start.11 = (bf16[80,8192]{1,0:T(8,128)(2,1)S(1)}, bf16[80,8192]{1,0:T(8,128)(2,1)S(1)}, u32[]{:S(2)}, u32[]{:S(2)}) collective-permute-start(bf16[80,8192]{1,0:T(8,128)(2,1)S(1)} %norm_backward.2.rest_0_), channel_id=1, source_target_pairs={{8,0},{16,8},{24,16},{9,1},{17,9},{25,17},{10,2},{18,10},{26,18},{... | collective-permute-start | bytes 3932168 | tf_op jit(solution)/shard_map/ppermute | solution.py:25
  91.8 38.9 %collective-permute-start.16 = (bf16[96,2560]{1,0:T(8,128)(2,1)S(1)}, bf16[96,2560]{1,0:T(8,128)(2,1)S(1)}, u32[]{:S(2)}, u32[]{:S(2)}) collective-permute-start(bf16[96,2560]{1,0:T(8,128)(2,1)S(1)} %norm_forward.6.rest_0_), channel_id=1, source_target_pairs={{0,4},{1,5},{2,6},{3,7},{4,0},{5,1},{6,2},{7,3},{8,12},{9,13},{10,... | collective-permute-start | bytes 1474568 | tf_op jit(solution)/shard_map/ppermute | solution.py:34
  93.3 33.0 %collective-permute-start.17 = (bf16[128,2560]{1,0:T(8,128)(2,1)S(1)}, bf16[128,2560]{1,0:T(8,128)(2,1)S(1)}, u32[]{:S(2)}, u32[]{:S(2)}) collective-permute-start(bf16[128,2560]{1,0:T(8,128)(2,1)S(1)} %norm_forward.7.rest_4_), channel_id=1, source_target_pairs={{0,6},{1,7},{2,0},{3,1},{4,2},{5,3},{6,4},{7,5},{8,14},{9,15},{10,... | collective-permute-start | bytes 1966088 | tf_op jit(solution)/shard_map/ppermute | solution.py:34
  93.7 21.7 %collective-permute-start.19 = (bf16[32,2560]{1,0:T(8,128)(2,1)S(1)}, bf16[32,2560]{1,0:T(8,128)(2,1)S(1)}, u32[]{:S(2)}, u32[]{:S(2)}) collective-permute-start(bf16[32,2560]{1,0:T(8,128)(2,1)S(1)} %get-tuple-element.24), channel_id=1, source_target_pairs={{0,8},{1,9},{2,10},{3,11},{4,12},{5,13},{6,14},{7,15}} | collective-permute-start | bytes 491528 | tf_op jit(solution)/shard_map/ppermute | solution.py:40
  114.7 3.1 %collective-permute-start.20 = (bf16[32,2560]{1,0:T(8,128)(2,1)S(1)}, bf16[32,2560]{1,0:T(8,128)(2,1)S(1)}, u32[]{:S(2)}, u32[]{:S(2)}) collective-permute-start(bf16[32,2560]{1,0:T(8,128)(2,1)S(1)} %get-tuple-element.23), channel_id=1, source_target_pairs={{0,16},{1,17},{2,18},{3,19},{4,20},{5,21},{6,22},{7,23}} | collective-permute-start | bytes 491528 | tf_op jit(solution)/shard_map/ppermute | solution.py:40
  115.4 8.6 %collective-permute-start.21 = (bf16[32,2560]{1,0:T(8,128)(2,1)S(1)}, bf16[32,2560]{1,0:T(8,128)(2,1)S(1)}, u32[]{:S(2)}, u32[]{:S(2)}) collective-permute-start(bf16[32,2560]{1,0:T(8,128)(2,1)S(1)} %get-tuple-element.22), channel_id=1, source_target_pairs={{0,24},{1,25},{2,26},{3,27},{4,28},{5,29},{6,30},{7,31}} | collective-permute-start | bytes 491528 | tf_op jit(solution)/shard_map/ppermute | solution.py:40
  117.8 17.5 %collective-permute-start.15 = (bf16[48,8192]{1,0:T(8,128)(2,1)S(1)}, bf16[48,8192]{1,0:T(8,128)(2,1)S(1)}, u32[]{:S(2)}, u32[]{:S(2)}) collective-permute-start(bf16[48,8192]{1,0:T(8,128)(2,1)S(1)} %norm_backward.3.refs_14_), channel_id=1, source_target_pairs={{8,0},{16,8},{24,16},{9,1},{17,9},{25,17},{10,2},{18,10},{26,18},{... | collective-permute-start | bytes 2359304 | tf_op jit(solution)/shard_map/ppermute | solution.py:25
  131.3 5.5 %collective-permute-start.23 = (bf16[512,512]{1,0:T(8,128)(2,1)S(1)}, bf16[512,512]{1,0:T(8,128)(2,1)S(1)}, u32[]{:S(2)}, u32[]{:S(2)}) collective-permute-start(bf16[512,512]{1,0:T(8,128)(2,1)S(1)} %outer.8), channel_id=1, source_target_pairs={{0,1},{1,0},{2,3},{3,2},{4,5},{5,4},{6,7},{7,6},{8,9},{9,8},{10,11... | collective-permute-start | bytes 1572872 | tf_op jit(solution)/shard_map/ppermute | solution.py:51
  131.9 4.8 %collective-permute-start.22 = (bf16[512,512]{1,0:T(8,128)(2,1)S(1)}, bf16[512,512]{1,0:T(8,128)(2,1)S(1)}, u32[]{:S(2)}, u32[]{:S(2)}) collective-permute-start(bf16[512,512]{1,0:T(8,128)(2,1)S(1)} %outer.7), channel_id=1, source_target_pairs={{0,1},{1,0},{2,3},{3,2},{4,5},{5,4},{6,7},{7,6},{8,9},{9,8},{10,11... | collective-permute-start | bytes 1572872 | tf_op jit(solution)/shard_map/ppermute | solution.py:51
  136.8 1.6 %copy-start.3 = (bf16[128,8192]{1,0:T(8,128)(2,1)S(1)}, bf16[128,8192]{1,0:T(8,128)(2,1)}, u32[]{:S(2)}) copy-start(bf16[128,8192]{1,0:T(8,128)(2,1)} %stack_rows.3.refs_5_) | copy-start | bytes 6291460
